TPU v7x, 256 devices: a whole 4x4x8 slice. The times are simulated.
256 devices in a mesh: fsdp: 32 (over x, y, core), tensor: 8 (over z).
Axes of the slice: x: 4, y: 4, z: 8, core: 2. Of those that a mesh axis runs over, the one named last changes fastest.
Arguments:
- momentum: bfloat16 [8192, 26624], P('fsdp', 'tensor'), may hold values from -6 to 6
- gradient: bfloat16 [8192, 26624], P('fsdp', 'tensor'), may hold values from -6 to 6
- weight: bfloat16 [8192, 26624], P('fsdp', 'tensor'), may hold values from -6 to 6
- basis: bfloat16 [26624, 256], P('tensor'), may hold values from -0.0390625 to 0.0390625
Outputs:
- momentum_new: bfloat16 [8192, 26624], P('fsdp', 'tensor')
- weight_new: bfloat16 [8192, 26624], P('fsdp', 'tensor')
- basis_new: bfloat16 [26624, 256], P('tensor')
All inputs are finite; a program needn't handle non-finite values.
Results may differ from a plain program's by a relative error of at most 0.0061.
Values may be sent and summed in bfloat16 or wider, within the bound.
No kernel may reach another device: no remote copies, remote signals or barrier semaphores. Data moves between devices by JAX's collectives and lax.ppermute only.
A program may use at most 64 MiB of HBM per device.

v0:
```python
import math

import jax
import jax.numpy as jnp
from jax import lax
from jax.sharding import PartitionSpec as P

D = 8192
FF = 26624
RANK = 256


def local(momentum, gradient, weight, basis):
    summed = momentum.astype(jnp.float32) + gradient.astype(jnp.float32)
    summed_b = summed.astype(jnp.bfloat16)
    proj = lax.psum(jnp.dot(summed_b, basis, preferred_element_type=jnp.float32), "tensor")
    gram = lax.psum(jnp.dot(proj.T, proj, precision=lax.Precision.HIGHEST), "fsdp")
    lower = jnp.linalg.cholesky(gram)
    ortho = lax.linalg.triangular_solve(
        lower, proj, left_side=False, lower=True, transpose_a=True
    ).astype(jnp.bfloat16)
    partial_right = lax.dot_general(
        summed_b, ortho, (((0,), (0,)), ((), ())), preferred_element_type=jnp.float32
    )
    right = lax.psum(partial_right, "fsdp")
    colsq = lax.psum(jnp.sum(right * right, axis=0), "tensor")
    basis_new = (right * lax.rsqrt(colsq + 1e-06)).astype(jnp.bfloat16)
    right_b = right.astype(jnp.bfloat16)
    back = lax.dot_general(
        ortho, right_b, (((1,), (1,)), ((), ())), preferred_element_type=jnp.float32
    )
    momentum_new = (summed - 0.05 * back).astype(jnp.bfloat16)
    update = lax.dot_general(
        ortho, basis_new, (((1,), (1,)), ((), ())), preferred_element_type=jnp.float32
    )
    factor = 0.2 * math.sqrt(D * FF / RANK)
    weight_new = (weight.astype(jnp.float32) - factor * update).astype(jnp.bfloat16)
    return (momentum_new, weight_new, basis_new)


def solution(mesh):
    placed = (P("fsdp", "tensor"), P("fsdp", "tensor"), P("fsdp", "tensor"), P("tensor", None))
    return jax.shard_map(
        local,
        mesh=mesh,
        in_specs=placed,
        out_specs=(P("fsdp", "tensor"), P("fsdp", "tensor"), P("tensor", None)),
        check_vma=False,
    )
```

profile of v0, /device:TPU:33, one launch (start us, length us, event | category | flops | bytes accessed | tf_op | source)
XLA Modules:
  0.0 430.2 jit_solution(5639892407178623028)
XLA Ops:
  7.2 1.4 copy-done
  8.6 3.3 fusion.8
  12.0 70.2 %all-reduce.5.cloned.1.call-done = f32[256,256]{1,0:T(8,128)} async-done(((f32[256,256]{1,0:T(8,128)}), f32[256,256]{1,0:T(8,128)}) %all-reduce.5.cloned.1.call-update) | async-done | bytes 262160 | tf_op jit(solution)/shard_map/psum | solution.py:16
  82.2 2.3 fusion.22
  84.6 116.5 %all-reduce.7.cloned.1.call-done = f32[256,256]{0,1:T(8,128)} async-done(((f32[256,256]{0,1:T(8,128)}), f32[256,256]{0,1:T(8,128)}) %all-reduce.7.cloned.1.call-update) | async-done | bytes 262160 | tf_op jit(solution)/shard_map/psum | solution.py:17
  201.1 1.1 copy.8
  202.2 1.0 fusion.10
  203.2 0.7 copy-done.6
  203.9 11.7 %cholesky.50 = f32[128,128]{1,0:T(8,128)S(1)} custom-call(f32[128,128]{1,0:T(8,128)S(1)} %cholesky.118), custom_call_target="Cholesky" | custom-call | tf_op jit(solution)/shard_map/jit(cholesky)/cholesky | solution.py:18
  215.7 9.8 %custom-call.14 = f32[1,128,128]{1,2,0:T(8,128)S(1)} custom-call(f32[1,128,128]{2,1,0:T(8,128)S(1)} %get-tuple-element.24), custom_call_target="InvertDiagBlocksLowerTriangular" | custom-call | tf_op jit(solution)/shard_map/jit(cholesky)/cholesky | solution.py:18
  225.5 0.7 cholesky.113
  226.2 1.7 constant_dynamic-update-slice_fusion.1
  227.9 1.1 convolution_subtract_fusion.1
  229.0 11.7 %cholesky.105 = f32[128,128]{1,0:T(8,128)S(1)} custom-call(f32[128,128]{1,0:T(8,128)S(1)} %convolution_subtract_fusion.1), custom_call_target="Cholesky" | custom-call | tf_op jit(solution)/shard_map/jit(cholesky)/cholesky | solution.py:18
  240.7 0.6 select_reduce_fusion
  241.3 0.7 compare_reduce_fusion
  243.3 1.7 select_select_fusion
  245.1 6.9 %while.1 = (s32[]{:T(128)}, f32[256,256]{1,0:T(8,128)}, s32[2,2]{1,0:T(2,128)S(1)}, f32[2,128,128]{2,1,0:T(8,128)}, s32[]{:T(128)}) while((s32[]{:T(128)}, f32[256,256]{1,0:T(8,128)}, s32[2,2]{1,0:T(2,128)S(1)}, f32[2,128,128]{2,1,0:T(8,128)}, s32[]{:T(128)}) %tuple.28), condition=%wide.while_cond, body=%wide.while_body.sunk | while | flops 2 | bytes 132205 | solution.py:19
  245.7 2.9 bitcast_dynamic-update-slice_fusion.2
  249.2 2.8 bitcast_dynamic-update-slice_fusion.2
  252.0 21.1 %custom-call.15 = f32[2,128,128]{1,2,0:T(8,128)} custom-call(f32[2,128,128]{2,1,0:T(8,128)} %get-tuple-element.10), custom_call_target="InvertDiagBlocksLowerTriangular" | custom-call | tf_op jit(solution)/shard_map/triangular_solve | solution.py:19
  273.1 1.2 fusion.21
  274.3 1.3 convolution_subtract_fusion
  275.7 1.2 convolution_convert_fusion
  276.8 3.9 fusion.6
  280.8 119.7 %all-reduce.9.cloned.1.call-done = f32[3328,256]{1,0:T(8,128)} async-done(((f32[3328,256]{1,0:T(8,128)}), f32[3328,256]{1,0:T(8,128)}) %all-reduce.9.cloned.1.call-update) | async-done | bytes 3407888 | tf_op jit(solution)/shard_map/psum | solution.py:25
  400.5 2.4 multiply_reduce_fusion
  402.9 12.3 %psum.31 = f32[256]{0:T(256)S(1)} all-reduce(f32[256]{0:T(256)S(1)} %multiply_reduce_fusion), channel_id=1, replica_groups=mesh['fsdp'=32,'tensor'=8] {'tensor'}, use_global_device_ids=true, to_apply=%region_8.9 | all-reduce | flops 256 | bytes 2048 | tf_op jit(solution)/shard_map/psum | solution.py:26
  415.2 2.4 multiply_convert_fusion
  417.7 1.9 fusion.3
  419.6 1.3 copy-done.1
  421.4 2.2 fusion.2
  (27 shorter events, 2.1 us)
Async XLA Ops:
  7.2 1.5 copy-start
  7.2 75.0 %all-reduce.5.cloned.1.call-start = ((), (), s32[]{:S(2)}) async-start(), calls=%async_computation | async-start | bytes 524288 | tf_op jit(solution)/shard_map/psum | solution.py:16
  11.9 189.2 %all-reduce.7.cloned.1.call-start = ((), (), s32[]{:S(2)}) async-start(), calls=%async_computation.1 | async-start | bytes 524288 | tf_op jit(solution)/shard_map/psum | solution.py:17
  84.6 315.9 %all-reduce.9.cloned.1.call-start = ((), (), s32[]{:S(2)}) async-start(), calls=%async_computation.2 | async-start | bytes 6815744 | tf_op jit(solution)/shard_map/psum | solution.py:25
  203.2 0.7 copy-start.6
  225.5 51.4 %copy-start.2 = (bf16[256,3328]{1,0:T(8,128)(2,1)S(1)}, bf16[256,3328]{1,0:T(8,128)(2,1)}, u32[]{:S(2)}) copy-start(bf16[256,3328]{1,0:T(8,128)(2,1)} %param.5) | copy-start | bytes 5111812
  415.2 2.5 copy-start.5
  417.7 1.9 copy-start.4
  417.7 3.2 copy-start.1
  417.7 3.7 copy-start.3
Sparse Core Ops, SparseCore 0:
  12.1 70.1 all-reduce.4
  86.3 114.7 all-reduce.6
  280.9 119.5 all-reduce.8
where the time goes:
time: 437 us; the launch traced here: 430 us
  waiting for transfers between devices  306 us (70%)
  other arithmetic  63.2 us (14%)
  matrix products  20.1 us (5%)
  between operations  15.1 us (3%)
  local copies, waits for them, and re-layouts  12.8 us (3%)
  blocking collectives  12.3 us (3%)
    psum x1, waiting for transfers between devices, local(): right = lax.psum(partial_right, 'fsdp')  120 us
    psum x1, waiting for transfers between devices, local(): lax.psum(jnp.dot(proj.T, proj, precision=lax.Precision.HIGHEST), 'fsdp')  116 us
    psum x1, waiting for transfers between devices, local(): lax.psum(jnp.dot(summed_b, basis, preferred_element_type=jnp.float32), 't...  70.2 us
    another operation x6, other arithmetic, local(): lower = jnp.linalg.cholesky(gram)  34.6 us
    another operation x3, other arithmetic, local(): lax.linalg.triangular_solve(lower, proj, left_side=False, lower=True, tra...  22.8 us
    psum x1, blocking collectives, local(): colsq = lax.psum(jnp.sum(right * right, axis=0), 'tensor')  12.3 us
  transfers between devices with their start and end apart: 3, of which 3 were waited for; matrix products, arithmetic and copies ran while one was open for 0% of the time, Pallas kernels for 0%

commit v1 on v0

v1 whole, which is shorter than its diff:
```python
import math

import jax
import jax.numpy as jnp
from jax import lax
from jax.experimental import pallas as pl
from jax.experimental.pallas import tpu as pltpu
from jax.sharding import PartitionSpec as P

D = 8192
FF = 26624
RANK = 256
HALF = RANK // 2
F, T = "fsdp", "tensor"
HIGH = lax.Precision.HIGHEST
f32, bf16 = jnp.float32, jnp.bfloat16


def place(x, y, c):
    return ((x % 4) * 4 + y % 4) * 2 + c


def moves(fn):
    return [(place(x, y, c), place(*fn(x, y, c))) for x in range(4) for y in range(4) for c in range(2)]


CORE = moves(lambda x, y, c: (x, y, 1 - c))
YS = [moves(lambda x, y, c, k=k: (x, y + k, c)) for k in (1, 2, 3)]
XS = [moves(lambda x, y, c, k=k: (x + k, y, c)) for k in (1, 2, 3)]
ZS = [[(i, i ^ 1) for i in range(8)], [(i, i ^ 2) for i in range(8)], [(i, 7 - i) for i in range(8)]]
PLANE = [[place(x, y, c) for x in range(4) for y in range(4)] for c in range(2)]


def ring_sum(v, shifts):
    one, two, three = [lax.ppermute(v, F, s) for s in shifts]
    return (v + two) + (one + three)


def inverse_kernel(g_ref, w_ref, a_ref):
    n = RANK
    row = lax.broadcasted_iota(jnp.int32, (n, n), 0)
    col = lax.broadcasted_iota(jnp.int32, (n, n), 1)
    eye = row == col
    g = g_ref[...]
    on_diag = jnp.where(eye, g, 0.0)
    d_row = lax.rsqrt(jnp.sum(on_diag, axis=0, keepdims=True))
    d_col = lax.rsqrt(jnp.sum(on_diag, axis=1, keepdims=True))

    def correction(c):
        return jnp.where(row > col, c, 0.0) + jnp.where(eye, 0.5 * (c - 1.0), 0.0)

    ident = jnp.where(eye, 1.0, 0.0)
    w_ref[...] = (ident - correction(g * d_col * d_row)) * d_row

    def dot(a, b, dims):
        return lax.dot_general(a, b, (dims, ((), ())), precision=HIGH, preferred_element_type=f32)

    def step(state):
        k, _ = state
        w = w_ref[...]
        c = dot(dot(w, g_ref[...], ((1,), (0,))), w, ((1,), (1,)))
        off = c - ident
        w_ref[...] = w - dot(correction(c), w, ((1,), (0,)))
        return k + 1, jnp.sum(off * off)

    _, err = lax.while_loop(
        lambda s: jnp.logical_and(s[0] < 9, jnp.logical_not(s[1] < 1e-6)), step, (0, jnp.float32(1.0))
    )

    @pl.when(jnp.logical_not(err < 1e-6))
    def _():
        a_ref[...] = g_ref[...]
        w_ref[...] = ident

        def eliminate(j, carry):
            a_row = a_ref[pl.ds(j, 1), :]
            lane = lax.broadcasted_iota(jnp.int32, (1, n), 1)
            pivot = jnp.sum(jnp.where(lane == j, a_row, 0.0), axis=1, keepdims=True)
            a = a_ref[...]
            column = jnp.sum(jnp.where(col == j, a, 0.0), axis=1, keepdims=True)
            down = lax.broadcasted_iota(jnp.int32, (n, 1), 0)
            factor = jnp.where(down > j, column / pivot, 0.0)
            w_row = w_ref[pl.ds(j, 1), :]
            a_ref[...] = a - factor * a_row
            w_ref[...] = w_ref[...] - factor * w_row
            w_ref[pl.ds(j, 1), :] = w_row * lax.rsqrt(pivot)
            return carry

        lax.fori_loop(0, n, eliminate, 0)


def inverse_factor(gram):
    return pl.pallas_call(
        inverse_kernel,
        out_shape=jax.ShapeDtypeStruct((RANK, RANK), f32),
        scratch_shapes=[pltpu.VMEM((RANK, RANK), f32)],
        compiler_params=pltpu.CompilerParams(vmem_limit_bytes=16 * 1024 * 1024),
        name="inverse_factor",
    )(gram)


def local(momentum, gradient, weight, basis):
    core = lax.axis_index(F) % 2

    def join(own, other):
        return jnp.where(
            core == 0, jnp.concatenate([own, other], axis=-1), jnp.concatenate([other, own], axis=-1)
        )

    def share(v):
        return lax.dynamic_slice_in_dim(v, core * HALF, HALF, axis=-1)

    summed = momentum.astype(f32) + gradient.astype(f32)
    summed_b = summed.astype(bf16)
    summed_o = lax.ppermute(summed_b, F, CORE)

    part = jnp.dot(summed_b, basis, preferred_element_type=f32)
    rows = jnp.sum(lax.all_to_all(part.reshape(8, 32, RANK), T, 0, 0), axis=0)
    proj = lax.all_to_all(jnp.broadcast_to(rows, (8, 32, RANK)), T, 0, 0).reshape(256, RANK)
    proj_o = lax.ppermute(proj, F, CORE)

    both = jnp.concatenate([proj, proj_o], axis=0)
    mine = share(both)
    gram = lax.dot_general(mine, both, (((0,), (0,)), ((), ())), precision=HIGH, preferred_element_type=f32)
    gram = ring_sum(ring_sum(gram, YS), XS)
    gram_o = lax.ppermute(gram, F, CORE)
    gram = jnp.where(
        core == 0, jnp.concatenate([gram, gram_o], axis=0), jnp.concatenate([gram_o, gram], axis=0)
    )
    inv = inverse_factor(gram)

    high = mine.astype(bf16)
    low = (mine - high.astype(f32)).astype(bf16)
    split = jnp.concatenate([high, low], axis=1)
    over_rows = (((0,), (0,)), ((), ()))
    u = lax.dot_general(summed_b, split[:256], over_rows, preferred_element_type=f32) + lax.dot_general(
        summed_o, split[256:], over_rows, preferred_element_type=f32
    )
    u = u[:, :HALF] + u[:, HALF:]
    u = lax.all_to_all(u.reshape(16, 208, HALF), F, 0, 0, axis_index_groups=PLANE)
    u = jnp.sum(u, axis=0)
    u = join(u, lax.ppermute(u, F, CORE))

    over_rank = (((1,), (1,)), ((), ()))
    right = lax.dot_general(u, inv, over_rank, precision=HIGH, preferred_element_type=f32)
    ortho = lax.dot_general(proj, inv, over_rank, precision=HIGH, preferred_element_type=f32).astype(bf16)
    right = share(right).astype(bf16)
    right = lax.all_to_all(
        jnp.broadcast_to(right, (16, 208, HALF)), F, 0, 0, axis_index_groups=PLANE
    ).reshape(3328, HALF)
    right_b = join(right, lax.ppermute(right, F, CORE))
    wide = right_b.astype(f32)
    colsq = jnp.sum(wide * wide, axis=0, keepdims=True)
    for s in ZS:
        colsq = colsq + lax.ppermute(colsq, T, s)
    basis_new = (wide * lax.rsqrt(colsq + 1e-06)).astype(bf16)
    back = lax.dot_general(ortho, right_b, over_rank, preferred_element_type=f32)
    momentum_new = (summed - 0.05 * back).astype(bf16)
    update = lax.dot_general(ortho, basis_new, over_rank, preferred_element_type=f32)
    factor = 0.2 * math.sqrt(D * FF / RANK)
    weight_new = (weight.astype(f32) - factor * update).astype(bf16)
    return (momentum_new, weight_new, basis_new)


def solution(mesh):
    placed = (P(F, T), P(F, T), P(F, T), P(T, None))
    return jax.shard_map(
        local,
        mesh=mesh,
        in_specs=placed,
        out_specs=(P(F, T), P(F, T), P(T, None)),
        check_vma=False,
    )
```

time: 437 us -> 189 us (0.43)
  waiting for transfers between devices: 306 us -> 37.7 us
  other arithmetic: 63.2 us -> 10.3 us
  Pallas kernels: 0 us -> 49.9 us
  blocking collectives: 12.3 us -> 49.2 us
  starting transfers between devices: 0.12 us -> 24.8 us
  between operations: 15.1 us -> 0.79 us
  local copies, waits for them, and re-layouts: 12.8 us -> 0.43 us
  matrix products: 20.1 us -> 12 us
    psum x3 -> x0, waiting for transfers between devices: 306 us -> none  [the longest x1 120 us: local(): right = lax.psum(partial_right, 'fsdp')]
    another operation x9 -> x0, other arithmetic: 57.4 us -> none  [the longest x6 34.6 us: local(): lower = jnp.linalg.cholesky(gram)]
    pallas_call x0 -> x1, Pallas kernels: none -> 49.9 us  [inverse_factor(): pl.pallas_call(inverse_kernel, out_shape=jax.ShapeDtypeStruct((RANK, RANK...]
    all_to_all x0 -> x3, blocking collectives: none -> 49.2 us  [the longest x1 17.1 us: local(): rows = jnp.sum(lax.all_to_all(part.reshape(8, 32, RANK), T, 0, 0), axis=0)]
    ppermute x0 -> x14, waiting for transfers between devices: none -> 37.7 us  [the longest x6 28.5 us: ring_sum(): one, two, three = [lax.ppermute(v, F, s) for s in shifts]]
    ppermute x0 -> x14, starting transfers between devices: none -> 18 us  [the longest x6 9.14 us: ring_sum(): one, two, three = [lax.ppermute(v, F, s) for s in shifts]]
    psum x1 -> x0, blocking collectives: 12.3 us -> none  [local(): colsq = lax.psum(jnp.sum(right * right, axis=0), 'tensor')]
    another operation x9 -> x0, local copies, waits for them, and re-layouts: 7.71 us -> none
  transfers between devices with their start and end apart: 3 -> 15, of which waited for: 3 -> 11; matrix products, arithmetic and copies ran while one was open for 0% -> 6% of each run, Pallas kernels for 0% -> 27%
where the time goes in v1:
time: 189 us; the launch traced here: 185 us
  Pallas kernels  49.9 us (26%)
  blocking collectives  49.2 us (26%)
  waiting for transfers between devices  37.7 us (20%)
  starting transfers between devices  24.8 us (13%)
  matrix products  12 us (6%)
  other arithmetic  10.3 us (5%)
    pallas_call x1, Pallas kernels, inverse_factor(): pl.pallas_call(inverse_kernel, out_shape=jax.ShapeDtypeStruct((RANK, RANK...  49.9 us
    ppermute x6, waiting for transfers between devices, ring_sum(): one, two, three = [lax.ppermute(v, F, s) for s in shifts]  28.5 us
    all_to_all x1, blocking collectives, local(): rows = jnp.sum(lax.all_to_all(part.reshape(8, 32, RANK), T, 0, 0), axis=0)  17.1 us
    all_to_all x1, blocking collectives, local(): lax.all_to_all(jnp.broadcast_to(right, (16, 208, HALF)), F, 0, 0, axis_in...  16.9 us
    all_to_all x1, blocking collectives, local(): lax.all_to_all(jnp.broadcast_to(rows, (8, 32, RANK)), T, 0, 0)  15.2 us
    ppermute x6, starting transfers between devices, ring_sum(): one, two, three = [lax.ppermute(v, F, s) for s in shifts]  9.14 us
    all_to_all x1, starting transfers between devices, local(): lax.all_to_all(u.reshape(16, 208, HALF), F, 0, 0, axis_index_groups=PLANE)  6.76 us
    ppermute x3, waiting for transfers between devices, local(): colsq = colsq + lax.ppermute(colsq, T, s)  5.37 us
  transfers between devices with their start and end apart: 15, of which 11 were waited for; matrix products, arithmetic and copies ran while one was open for 6% of the time, Pallas kernels for 27%

profile of v1, /device:TPU:33, one launch (start us, length us, event | category | flops | bytes accessed | tf_op | source)
XLA Modules:
  0.0 185.1 jit_solution(2953968209259466809)
XLA Ops:
  0.6 2.5 %fusion.6 = bf16[256,3328]{1,0:T(8,128)(2,1)S(1)} fusion(bf16[256,3328]{1,0:T(8,128)(2,1)} %param.5, bf16[256,3328]{1,0:T(8,128)(2,1)} %param.4), kind=kLoop, calls=%fused_computation.12 | loop fusion | flops 3407872 | bytes 5111808 | tf_op jit(solution)/shard_map/convert_element_type | solution.py:114
  4.5 17.1 %all_to_all.20 = f32[8,32,256]{2,1,0:T(8,128)} all-to-all(f32[8,32,256]{2,1,0:T(8,128)S(1)} %bitcast.21), channel_id=1, replica_groups=mesh['fsdp'=32,'tensor'=8] {'tensor'}, dimensions={0} | all-to-all | bytes 524288 | tf_op jit(solution)/shard_map/all_to_all | solution.py:118
  22.6 15.2 %all_to_all.21 = f32[8,32,256]{2,1,0:T(8,128)} all-to-all(f32[8,32,256]{2,1,0:T(8,128)S(1)} %broadcast_in_dim.9), channel_id=1, replica_groups=mesh['fsdp'=32,'tensor'=8] {'tensor'}, dimensions={0} | all-to-all | bytes 524288 | tf_op jit(solution)/shard_map/all_to_all | solution.py:119
  37.8 2.7 %collective-permute-start = (f32[256,256]{1,0:T(8,128)}, f32[256,256]{1,0:T(8,128)}, u32[]{:S(2)}, u32[]{:S(2)}) collective-permute-start(f32[256,256]{1,0:T(8,128)} %bitcast.1), channel_id=1, source_target_pairs={{0,8},{8,0},{16,24},{24,16},{32,40},{40,32},{48,56},{56,48},{64,72... | collective-permute-start | bytes 786440 | tf_op jit(solution)/shard_map/ppermute | solution.py:120
  40.5 1.5 collective-permute-done
  42.0 1.7 subtract_convert_fusion
  44.4 2.2 %convolution_add_fusion = f32[3328,256]{1,0:T(8,128)S(1)} fusion(f32[3328,256]{1,0:T(8,128)S(1)} %fusion.16, bf16[256,3328]{1,0:T(8,128)(2,1)} %collective-permute-done.8, bf16[512,128]{1,0:T(8,128)(2,1)S(1)} %get-tuple-element.3, bf16[512,128]{1,0:T(8,128)(2,1)S(1)} %get-tuple-element.4), kind=kOutput, calls=%fused_computation.4 | convolution fusion | flops 437321728 | bytes 8781824 | tf_op jit(solution)/shard_map/dot_general | solution.py:136
  46.6 1.4 slice_add_fusion
  47.9 6.8 %all-to-all-start.2 = ((f32[16,208,128]{2,1,0:T(8,128)}), f32[16,208,128]{2,1,0:T(8,128)S(1)}, u32[]{:S(2)}, u32[]{:S(2)}) async-start(f32[16,208,128]{2,1,0:T(8,128)} %bitcast.2), calls=%async_computation.2 | async-start | bytes 3407872 | tf_op jit(solution)/shard_map/all_to_all | solution.py:140
  54.7 1.7 fusion.7
  56.4 2.6 %collective-permute-start.3 = (f32[128,256]{1,0:T(8,128)S(1)}, f32[128,256]{1,0:T(8,128)S(1)}, u32[]{:S(2)}, u32[]{:S(2)}) collective-permute-start(f32[128,256]{1,0:T(8,128)S(1)} %fusion.7), channel_id=1, source_target_pairs={{0,48},{8,56},{16,0},{24,8},{32,16},{40,24},{48,32},{56,40},{64,11... | collective-permute-start | bytes 393224 | tf_op jit(solution)/shard_map/ppermute | solution.py:35
  59.0 1.8 collective-permute-start.1
  60.8 16.6 %collective-permute-done.3 = f32[128,256]{1,0:T(8,128)S(1)} collective-permute-done((f32[128,256]{1,0:T(8,128)S(1)}, f32[128,256]{1,0:T(8,128)S(1)}, u32[]{:S(2)}, u32[]{:S(2)}) %collective-permute-start.3) | collective-permute-done | bytes 131104 | tf_op jit(solution)/shard_map/ppermute | solution.py:35
  77.4 1.9 %collective-permute-done.2 = f32[128,256]{1,0:T(8,128)S(1)} collective-permute-done((f32[128,256]{1,0:T(8,128)S(1)}, f32[128,256]{1,0:T(8,128)S(1)}, u32[]{:S(2)}, u32[]{:S(2)}) %collective-permute-start.2) | collective-permute-done | bytes 131104 | tf_op jit(solution)/shard_map/ppermute | solution.py:35
  79.3 2.5 %collective-permute-done.1 = f32[128,256]{1,0:T(8,128)S(1)} collective-permute-done((f32[128,256]{1,0:T(8,128)S(1)}, f32[128,256]{1,0:T(8,128)S(1)}, u32[]{:S(2)}, u32[]{:S(2)}) %collective-permute-start.1) | collective-permute-done | bytes 131104 | tf_op jit(solution)/shard_map/ppermute | solution.py:35
  81.9 3.5 %collective-permute-start.6 = (f32[128,256]{1,0:T(8,128)S(1)}, f32[128,256]{1,0:T(8,128)S(1)}, u32[]{:S(2)}, u32[]{:S(2)}) collective-permute-start(f32[128,256]{1,0:T(8,128)S(1)} %add_add_fusion.1), channel_id=1, source_target_pairs={{0,192},{8,200},{16,208},{24,216},{32,224},{40,232},{48,240},{56,2... | collective-permute-start | bytes 393224 | tf_op jit(solution)/shard_map/ppermute | solution.py:35
  85.3 1.3 collective-permute-start.4
  87.7 6.4 %collective-permute-done.5 = f32[128,256]{1,0:T(8,128)S(1)} collective-permute-done((f32[128,256]{1,0:T(8,128)S(1)}, f32[128,256]{1,0:T(8,128)S(1)}, u32[]{:S(2)}, u32[]{:S(2)}) %collective-permute-start.5) | collective-permute-done | bytes 131104 | tf_op jit(solution)/shard_map/ppermute | solution.py:35
  94.1 1.3 collective-permute-start.7
  97.5 49.9 %inverse_factor.1 = f32[256,256]{1,0:T(8,128)S(1)} custom-call(f32[256,256]{1,0:T(8,128)S(1)} %maximum_select_fusion.1.g_ref), custom_call_target="tpu_custom_call" | custom-call | tf_op jit(solution)/shard_map/inverse_factor/pallas_call | solution.py:93
  147.4 1.4 fusion.9
  149.0 16.9 %all_to_all.22 = bf16[16,208,128]{2,1,0:T(8,128)(2,1)S(1)} all-to-all(bf16[16,208,128]{2,1,0:T(8,128)(2,1)S(1)} %broadcast_in_dim.10), channel_id=1, replica_groups={{0,16,32,48,64,80,96,112,128,144,160,176,192,208,224,240},{8,24,40,56,7..., dimensions={0} | all-to-all | bytes 1703936 | tf_op jit(solution)/shard_map/all_to_all | solution.py:148
  165.9 1.8 collective-permute-start.10
  167.8 2.0 %collective-permute-done.10 = bf16[3328,128]{1,0:T(8,128)(2,1)S(1)} collective-permute-done((bf16[3328,128]{1,0:T(8,128)(2,1)S(1)}, bf16[3328,128]{1,0:T(8,128)(2,1)S(1)}, u32[]{:S(2)}, u32[]{:S(2)}) %collective-permute-start.10) | collective-permute-done | bytes 852000 | tf_op jit(solution)/shard_map/ppermute | solution.py:151
  170.5 1.3 collective-permute-start.11
  171.8 1.2 collective-permute-done.11
  173.0 1.4 convolution_convert_fusion
  174.4 1.9 %collective-permute-done.12 = f32[1,256]{1,0:T(1,128)S(1)} collective-permute-done((f32[1,256]{1,0:T(1,128)S(1)}, f32[1,256]{1,0:T(1,128)S(1)}, u32[]{:S(2)}, u32[]{:S(2)}) %collective-permute-start.12) | collective-permute-done | bytes 1056 | tf_op jit(solution)/shard_map/ppermute | solution.py:155
  177.3 2.3 %fusion.2 = bf16[256,3328]{1,0:T(8,128)(2,1)} fusion(bf16[256,256]{1,0:T(8,128)(2,1)S(1)} %convolution_convert_fusion, bf16[256,3328]{1,0:T(8,128)(2,1)S(1)} %copy-done.2, bf16[256,3328]{1,0:T(8,128)(2,1)S(1)} %copy-done.3, bf16[3328,128]{1,0:T(8,128)(2,1)S(1)} %collective-permute-done.10, bf16[3328,128]{1,0:T(8,128)(2,1)S(1)} %bitcast.19, pred[]{:T(512)S(6)} %eq.4), kind=kOutput, calls=%fused_computation.5 | convolution fusion | flops 448987136 | bytes 6946817 | tf_op jit(solution)/shard_map/dot_general | solution.py:157
  179.6 2.2 %collective-permute-done.13 = f32[1,256]{1,0:T(1,128)S(1)} collective-permute-done((f32[1,256]{1,0:T(1,128)S(1)}, f32[1,256]{1,0:T(1,128)S(1)}, u32[]{:S(2)}, u32[]{:S(2)}) %collective-permute-start.13) | collective-permute-done | bytes 1056 | tf_op jit(solution)/shard_map/ppermute | solution.py:155
  181.8 1.2 fusion.5
  183.2 1.8 fusion.3
  (36 shorter events, 8.5 us)
Async XLA Ops:
  0.6 3.3 %copy-start = (bf16[3328,256]{1,0:T(8,128)(2,1)S(1)}, bf16[3328,256]{1,0:T(8,128)(2,1)}, u32[]{:S(2)}) copy-start(bf16[3328,256]{1,0:T(8,128)(2,1)} %param.7) | copy-start | bytes 5111812
  3.1 41.3 %collective-permute-start.8 = (bf16[256,3328]{1,0:T(8,128)(2,1)S(1)}, bf16[256,3328]{1,0:T(8,128)(2,1)}, u32[]{:S(2)}, u32[]{:S(2)}) collective-permute-start(bf16[256,3328]{1,0:T(8,128)(2,1)S(1)} %fusion.6), channel_id=1, source_target_pairs={{0,8},{8,0},{16,24},{24,16},{32,40},{40,32},{48,56},{56,48},{64,72... | collective-permute-start | bytes 5111816 | tf_op jit(solution)/shard_map/ppermute | solution.py:115
  37.8 4.2 %collective-permute-start = (f32[256,256]{1,0:T(8,128)}, f32[256,256]{1,0:T(8,128)}, u32[]{:S(2)}, u32[]{:S(2)}) collective-permute-start(f32[256,256]{1,0:T(8,128)} %bitcast.1), channel_id=1, source_target_pairs={{0,8},{8,0},{16,24},{24,16},{32,40},{40,32},{48,56},{56,48},{64,72... | collective-permute-start | bytes 786440 | tf_op jit(solution)/shard_map/ppermute | solution.py:120
  47.9 47.5 %all-to-all-start.2 = ((f32[16,208,128]{2,1,0:T(8,128)}), f32[16,208,128]{2,1,0:T(8,128)S(1)}, u32[]{:S(2)}, u32[]{:S(2)}) async-start(f32[16,208,128]{2,1,0:T(8,128)} %bitcast.2), calls=%async_computation.2 | async-start | bytes 3407872 | tf_op jit(solution)/shard_map/all_to_all | solution.py:140
  56.4 21.0 %collective-permute-start.3 = (f32[128,256]{1,0:T(8,128)S(1)}, f32[128,256]{1,0:T(8,128)S(1)}, u32[]{:S(2)}, u32[]{:S(2)}) collective-permute-start(f32[128,256]{1,0:T(8,128)S(1)} %fusion.7), channel_id=1, source_target_pairs={{0,48},{8,56},{16,0},{24,8},{32,16},{40,24},{48,32},{56,40},{64,11... | collective-permute-start | bytes 393224 | tf_op jit(solution)/shard_map/ppermute | solution.py:35
  59.0 20.3 %collective-permute-start.2 = (f32[128,256]{1,0:T(8,128)S(1)}, f32[128,256]{1,0:T(8,128)S(1)}, u32[]{:S(2)}, u32[]{:S(2)}) collective-permute-start(f32[128,256]{1,0:T(8,128)S(1)} %fusion.7), channel_id=1, source_target_pairs={{0,16},{8,24},{16,32},{24,40},{32,48},{40,56},{48,0},{56,8},{64,80... | collective-permute-start | bytes 393224 | tf_op jit(solution)/shard_map/ppermute | solution.py:35
  59.0 22.8 %collective-permute-start.1 = (f32[128,256]{1,0:T(8,128)S(1)}, f32[128,256]{1,0:T(8,128)S(1)}, u32[]{:S(2)}, u32[]{:S(2)}) collective-permute-start(f32[128,256]{1,0:T(8,128)S(1)} %fusion.7), channel_id=1, source_target_pairs={{0,32},{8,40},{16,48},{24,56},{32,0},{40,8},{48,16},{56,24},{64,96... | collective-permute-start | bytes 393224 | tf_op jit(solution)/shard_map/ppermute | solution.py:35
  81.9 5.8 %collective-permute-start.6 = (f32[128,256]{1,0:T(8,128)S(1)}, f32[128,256]{1,0:T(8,128)S(1)}, u32[]{:S(2)}, u32[]{:S(2)}) collective-permute-start(f32[128,256]{1,0:T(8,128)S(1)} %add_add_fusion.1), channel_id=1, source_target_pairs={{0,192},{8,200},{16,208},{24,216},{32,224},{40,232},{48,240},{56,2... | collective-permute-start | bytes 393224 | tf_op jit(solution)/shard_map/ppermute | solution.py:35
  85.3 8.7 %collective-permute-start.5 = (f32[128,256]{1,0:T(8,128)S(1)}, f32[128,256]{1,0:T(8,128)S(1)}, u32[]{:S(2)}, u32[]{:S(2)}) collective-permute-start(f32[128,256]{1,0:T(8,128)S(1)} %add_add_fusion.1), channel_id=1, source_target_pairs={{0,64},{8,72},{16,80},{24,88},{32,96},{40,104},{48,112},{56,120},{... | collective-permute-start | bytes 393224 | tf_op jit(solution)/shard_map/ppermute | solution.py:35
  85.3 8.7 %collective-permute-start.4 = (f32[128,256]{1,0:T(8,128)S(1)}, f32[128,256]{1,0:T(8,128)S(1)}, u32[]{:S(2)}, u32[]{:S(2)}) collective-permute-start(f32[128,256]{1,0:T(8,128)S(1)} %add_add_fusion.1), channel_id=1, source_target_pairs={{0,128},{8,136},{16,144},{24,152},{32,160},{40,168},{48,176},{56,1... | collective-permute-start | bytes 393224 | tf_op jit(solution)/shard_map/ppermute | solution.py:35
  94.1 2.4 %collective-permute-start.7 = (f32[128,256]{1,0:T(8,128)S(1)}, f32[128,256]{1,0:T(8,128)}, u32[]{:S(2)}, u32[]{:S(2)}) collective-permute-start(f32[128,256]{1,0:T(8,128)S(1)} %add_add_fusion), channel_id=1, source_target_pairs={{0,8},{8,0},{16,24},{24,16},{32,40},{40,32},{48,56},{56,48},{64,72... | collective-permute-start | bytes 393224 | tf_op jit(solution)/shard_map/ppermute | solution.py:126
  96.1 51.3 %collective-permute-start.9 = (f32[208,128]{1,0:T(8,128)}, f32[208,128]{1,0:T(8,128)S(1)}, u32[]{:S(2)}, u32[]{:S(2)}) collective-permute-start(f32[208,128]{1,0:T(8,128)} %reduce_sum.28), channel_id=1, source_target_pairs={{0,8},{8,0},{16,24},{24,16},{32,40},{40,32},{48,56},{56,48},{64,72... | collective-permute-start | bytes 319496 | tf_op jit(solution)/shard_map/ppermute | solution.py:142
  149.0 28.3 %copy-start.2 = (bf16[256,3328]{1,0:T(8,128)(2,1)S(1)}, bf16[256,3328]{1,0:T(8,128)(2,1)}, u32[]{:S(2)}) copy-start(bf16[256,3328]{1,0:T(8,128)(2,1)} %param.5) | copy-start | bytes 5111812
  149.0 28.3 %copy-start.3 = (bf16[256,3328]{1,0:T(8,128)(2,1)S(1)}, bf16[256,3328]{1,0:T(8,128)(2,1)}, u32[]{:S(2)}) copy-start(bf16[256,3328]{1,0:T(8,128)(2,1)} %param.4) | copy-start | bytes 5111812
  165.9 3.9 %collective-permute-start.10 = (bf16[3328,128]{1,0:T(8,128)(2,1)S(1)}, bf16[3328,128]{1,0:T(8,128)(2,1)S(1)}, u32[]{:S(2)}, u32[]{:S(2)}) collective-permute-start(bf16[3328,128]{1,0:T(8,128)(2,1)S(1)} %bitcast.17), channel_id=1, source_target_pairs={{0,8},{8,0},{16,24},{24,16},{32,40},{40,32},{48,56},{56,48},{64,72... | collective-permute-start | bytes 2555912 | tf_op jit(solution)/shard_map/ppermute | solution.py:151
  170.5 2.5 %collective-permute-start.11 = (f32[1,256]{1,0:T(1,128)S(1)}, f32[1,256]{1,0:T(1,128)S(1)}, u32[]{:S(2)}, u32[]{:S(2)}) collective-permute-start(f32[1,256]{1,0:T(1,128)S(1)} %bitcast.23), channel_id=1, source_target_pairs={{0,1},{1,0},{2,3},{3,2},{4,5},{5,4},{6,7},{7,6},{8,9},{9,8},{10,11... | collective-permute-start | bytes 3080 | tf_op jit(solution)/shard_map/ppermute | solution.py:155
  173.0 3.3 %collective-permute-start.12 = (f32[1,256]{1,0:T(1,128)S(1)}, f32[1,256]{1,0:T(1,128)S(1)}, u32[]{:S(2)}, u32[]{:S(2)}) collective-permute-start(f32[1,256]{1,0:T(1,128)S(1)} %add.61), channel_id=1, source_target_pairs={{0,2},{1,3},{2,0},{3,1},{4,6},{5,7},{6,4},{7,5},{8,10},{9,11},{10,... | collective-permute-start | bytes 3080 | tf_op jit(solution)/shard_map/ppermute | solution.py:155
  176.3 5.4 %collective-permute-start.13 = (f32[1,256]{1,0:T(1,128)S(1)}, f32[1,256]{1,0:T(1,128)S(1)}, u32[]{:S(2)}, u32[]{:S(2)}) collective-permute-start(f32[1,256]{1,0:T(1,128)S(1)} %add.62), channel_id=1, source_target_pairs={{0,7},{1,6},{2,5},{3,4},{4,3},{5,2},{6,1},{7,0},{8,15},{9,14},{10,... | collective-permute-start | bytes 3080 | tf_op jit(solution)/shard_map/ppermute | solution.py:155
  181.8 1.5 copy-start.4
  183.2 1.8 copy-start.1

commit v2 on v1

--- a/solution.py
+++ b/solution.py
@@ -28,7 +28,9 @@
 YS = [moves(lambda x, y, c, k=k: (x, y + k, c)) for k in (1, 2, 3)]
 XS = [moves(lambda x, y, c, k=k: (x + k, y, c)) for k in (1, 2, 3)]
 ZS = [[(i, i ^ 1) for i in range(8)], [(i, i ^ 2) for i in range(8)], [(i, 7 - i) for i in range(8)]]
-PLANE = [[place(x, y, c) for x in range(4) for y in range(4)] for c in range(2)]
+YG = [[place(x, y, c) for y in range(4)] for x in range(4) for c in range(2)]
+XG = [[place(x, y, c) for x in range(4)] for y in range(4) for c in range(2)]
+PLANE = [[place(x, y, c) for y in range(4) for x in range(4)] for c in range(2)]
 
 
 def ring_sum(v, shifts):
@@ -36,8 +38,11 @@
     return (v + two) + (one + three)
 
 
-def inverse_kernel(g_ref, w_ref, a_ref):
+def inverse_kernel(core_ref, own_ref, other_ref, w_ref, g_ref, a_ref):
     n = RANK
+    first = core_ref[0] == 0
+    g_ref[:HALF, :] = jnp.where(first, own_ref[...], other_ref[...])
+    g_ref[HALF:, :] = jnp.where(first, other_ref[...], own_ref[...])
     row = lax.broadcasted_iota(jnp.int32, (n, n), 0)
     col = lax.broadcasted_iota(jnp.int32, (n, n), 1)
     eye = row == col
@@ -52,19 +57,23 @@
     ident = jnp.where(eye, 1.0, 0.0)
     w_ref[...] = (ident - correction(g * d_col * d_row)) * d_row
 
-    def dot(a, b, dims):
-        return lax.dot_general(a, b, (dims, ((), ())), precision=HIGH, preferred_element_type=f32)
+    def dot(a, b, dims, precision=HIGH):
+        return lax.dot_general(a, b, (dims, ((), ())), precision=precision, preferred_element_type=f32)
+
+    def refine(precision):
+        w = w_ref[...]
+        c = dot(dot(w, g_ref[...], ((1,), (0,)), precision), w, ((1,), (1,)), precision)
+        off = c - ident
+        w_ref[...] = w - dot(correction(c), w, ((1,), (0,)), lax.Precision.DEFAULT)
+        return jnp.sum(off * off)
 
     def step(state):
-        k, _ = state
-        w = w_ref[...]
-        c = dot(dot(w, g_ref[...], ((1,), (0,))), w, ((1,), (1,)))
-        off = c - ident
-        w_ref[...] = w - dot(correction(c), w, ((1,), (0,)))
-        return k + 1, jnp.sum(off * off)
+        return state[0] + 1, refine(HIGH)
+
+    refine(lax.Precision.DEFAULT)
 
     _, err = lax.while_loop(
-        lambda s: jnp.logical_and(s[0] < 9, jnp.logical_not(s[1] < 1e-6)), step, (0, jnp.float32(1.0))
+        lambda s: jnp.logical_and(s[0] < 10, jnp.logical_not(s[1] < 1e-6)), step, (0, jnp.float32(1.0))
     )
 
     @pl.when(jnp.logical_not(err < 1e-6))
@@ -89,14 +98,79 @@
         lax.fori_loop(0, n, eliminate, 0)
 
 
-def inverse_factor(gram):
+def inverse_factor(core, own, other):
+    block = pl.BlockSpec(memory_space=pltpu.VMEM)
     return pl.pallas_call(
         inverse_kernel,
         out_shape=jax.ShapeDtypeStruct((RANK, RANK), f32),
-        scratch_shapes=[pltpu.VMEM((RANK, RANK), f32)],
-        compiler_params=pltpu.CompilerParams(vmem_limit_bytes=16 * 1024 * 1024),
+        in_specs=[pl.BlockSpec(memory_space=pltpu.SMEM), block, block],
+        out_specs=block,
+        scratch_shapes=[pltpu.VMEM((RANK, RANK), f32)] * 2,
+        compiler_params=pltpu.CompilerParams(vmem_limit_bytes=4 * 1024 * 1024),
+        cost_estimate=pl.CostEstimate(flops=5_000_000_000, bytes_accessed=600_000, transcendentals=0),
         name="inverse_factor",
-    )(gram)
+    )(core, own, other)
+
+
+def assemble_kernel(place_ref, *refs):
+    pieces, (split_ref, gram_ref, proj_ref, other_ref, sems) = refs[:8], refs[8:]
+    first = place_ref[0] == 0
+    order = place_ref[1]
+    copies = []
+    for n, piece in enumerate(pieces):
+        at = pl.multiple_of(jnp.bitwise_xor(order, n % 4) * 64, 64)
+        target = (proj_ref if n < 4 else other_ref).at[pl.ds(at, 64), :]
+        copies.append(pltpu.make_async_copy(piece, target, sems.at[n]))
+    for copy in copies:
+        copy.start()
+    for copy in copies:
+        copy.wait()
+    grams = []
+    for at, ref in ((0, proj_ref), (256, other_ref)):
+        whole = ref[...]
+        mine = jnp.where(first, whole[:, :HALF], whole[:, HALF:])
+        high = mine.astype(bf16)
+        split_ref[at : at + 256, :HALF] = high
+        split_ref[at : at + 256, HALF:] = (mine - high.astype(f32)).astype(bf16)
+        grams.append(
+            lax.dot_general(mine, whole, (((0,), (0,)), ((), ())), precision=HIGH, preferred_element_type=f32)
+        )
+    gram_ref[...] = grams[0] + grams[1]
+
+
+def assemble(now, pieces):
+    vmem = pl.BlockSpec(memory_space=pltpu.VMEM)
+    return pl.pallas_call(
+        assemble_kernel,
+        in_specs=[pl.BlockSpec(memory_space=pltpu.SMEM)] + [pl.BlockSpec(memory_space=pl.ANY)] * 8,
+        out_specs=[vmem] * 3,
+        out_shape=[
+            jax.ShapeDtypeStruct((512, RANK), bf16),
+            jax.ShapeDtypeStruct((HALF, RANK), f32),
+            jax.ShapeDtypeStruct((256, RANK), f32),
+        ],
+        scratch_shapes=[pltpu.VMEM((256, RANK), f32), pltpu.SemaphoreType.DMA((8,))],
+        compiler_params=pltpu.CompilerParams(vmem_limit_bytes=4 * 1024 * 1024),
+        cost_estimate=pl.CostEstimate(flops=200_000_000, bytes_accessed=1_200_000, transcendentals=0),
+        name="assemble",
+    )(now, *pieces)
+
+
+def sum_over_z(part):
+    z = lax.axis_index(T)
+    label = jnp.where(z < 4, z, 7 - z)
+    low, mid = label % 2, label // 2
+    near = lambda v: lax.ppermute(v, T, ZS[0])
+    next_ = lambda v: lax.ppermute(v, T, ZS[1])
+    keep, send = low * 128 + mid * 64, low * 128 + (1 - mid) * 64
+    got = near(lax.dynamic_slice_in_dim(part, (1 - low) * 128, 128, 0))
+    out = lax.dynamic_slice_in_dim(part, send, 64, 0) + lax.dynamic_slice_in_dim(got, (1 - mid) * 64, 64, 0)
+    kept = lax.dynamic_slice_in_dim(part, keep, 64, 0) + lax.dynamic_slice_in_dim(got, mid * 64, 64, 0)
+    kept = kept + next_(out)
+    a = kept + lax.ppermute(kept, T, ZS[2])
+    b, c = next_(a), near(a)
+    d = near(b)
+    return (a, b, c, d), low * 2 + mid
 
 
 def local(momentum, gradient, weight, basis):
@@ -112,33 +186,39 @@
 
     summed = momentum.astype(f32) + gradient.astype(f32)
     summed_b = summed.astype(bf16)
+    part = jnp.dot(summed_b, basis, preferred_element_type=f32)
+    part, m2, g2 = lax.optimization_barrier((part, momentum, gradient))
+    summed_b = (m2.astype(f32) + g2.astype(f32)).astype(bf16)
     summed_o = lax.ppermute(summed_b, F, CORE)
-
-    part = jnp.dot(summed_b, basis, preferred_element_type=f32)
-    rows = jnp.sum(lax.all_to_all(part.reshape(8, 32, RANK), T, 0, 0), axis=0)
-    proj = lax.all_to_all(jnp.broadcast_to(rows, (8, 32, RANK)), T, 0, 0).reshape(256, RANK)
-    proj_o = lax.ppermute(proj, F, CORE)
-
-    both = jnp.concatenate([proj, proj_o], axis=0)
-    mine = share(both)
-    gram = lax.dot_general(mine, both, (((0,), (0,)), ((), ())), precision=HIGH, preferred_element_type=f32)
-    gram = ring_sum(ring_sum(gram, YS), XS)
-    gram_o = lax.ppermute(gram, F, CORE)
-    gram = jnp.where(
-        core == 0, jnp.concatenate([gram, gram_o], axis=0), jnp.concatenate([gram_o, gram], axis=0)
-    )
-    inv = inverse_factor(gram)
-
-    high = mine.astype(bf16)
-    low = (mine - high.astype(f32)).astype(bf16)
-    split = jnp.concatenate([high, low], axis=1)
+    pieces, order = sum_over_z(part)
+    others = [lax.ppermute(p, F, CORE) for p in pieces]
+    place_x, place_y = lax.axis_index(F) // 8, lax.axis_index(F) // 2 % 4
+
+    now = jnp.stack([core, order]).astype(jnp.int32)
+    split, gram, proj = assemble(now, [*pieces, *others])
     over_rows = (((0,), (0,)), ((), ()))
     u = lax.dot_general(summed_b, split[:256], over_rows, preferred_element_type=f32) + lax.dot_general(
         summed_o, split[256:], over_rows, preferred_element_type=f32
     )
-    u = u[:, :HALF] + u[:, HALF:]
-    u = lax.all_to_all(u.reshape(16, 208, HALF), F, 0, 0, axis_index_groups=PLANE)
-    u = jnp.sum(u, axis=0)
+
+    def along(v, k, here, size):
+        return lax.dynamic_slice_in_dim(v, (here + k) % 4 * size, size, 0)
+
+    us = []
+    for k in range(4):
+        w = along(u, k, place_y, 832)
+        us.append(w[:, :HALF] + w[:, HALF:])
+    us = [us[0]] + [lax.ppermute(us[k], F, YS[k - 1]) for k in (1, 2, 3)]
+    gram = ring_sum(gram, XS)
+    gram, us[0] = lax.optimization_barrier((gram, us[0]))
+    gram = ring_sum(gram, YS)
+    vs = []
+    for k in range(4):
+        w = [along(v, k, place_x, 208) for v in us]
+        vs.append((w[0] + w[2]) + (w[1] + w[3]))
+    u = vs[0] + lax.ppermute(vs[2], F, XS[1])
+    u = u + (lax.ppermute(vs[1], F, XS[0]) + lax.ppermute(vs[3], F, XS[2]))
+    inv = inverse_factor(now, gram, lax.ppermute(gram, F, CORE))
     u = join(u, lax.ppermute(u, F, CORE))
 
     over_rank = (((1,), (1,)), ((), ()))
@@ -149,13 +229,16 @@
         jnp.broadcast_to(right, (16, 208, HALF)), F, 0, 0, axis_index_groups=PLANE
     ).reshape(3328, HALF)
     right_b = join(right, lax.ppermute(right, F, CORE))
-    wide = right_b.astype(f32)
-    colsq = jnp.sum(wide * wide, axis=0, keepdims=True)
-    for s in ZS:
-        colsq = colsq + lax.ppermute(colsq, T, s)
-    basis_new = (wide * lax.rsqrt(colsq + 1e-06)).astype(bf16)
     back = lax.dot_general(ortho, right_b, over_rank, preferred_element_type=f32)
     momentum_new = (summed - 0.05 * back).astype(bf16)
+    colsq = jnp.sum(jnp.square(right.astype(f32)), axis=0, keepdims=True)
+    for i, s in enumerate(ZS):
+        got = lax.ppermute(colsq, T, s)
+        if i == 2:
+            got, momentum_new = lax.optimization_barrier((got, momentum_new))
+        colsq = colsq + got
+    colsq = join(colsq, lax.ppermute(colsq, F, CORE))
+    basis_new = (right_b.astype(f32) * lax.rsqrt(colsq + 1e-06)).astype(bf16)
     update = lax.dot_general(ortho, basis_new, over_rank, preferred_element_type=f32)
     factor = 0.2 * math.sqrt(D * FF / RANK)
     weight_new = (weight.astype(f32) - factor * update).astype(bf16)

time: 189 us -> 174 us (0.921); the launches traced: 185 us -> 174 us
  starting transfers between devices: 24.8 us -> 57.3 us
  blocking collectives: 49.2 us -> 17.6 us
  waiting for transfers between devices: 37.7 us -> 25.5 us
  other arithmetic: 10.3 us -> 7.02 us
  local copies, waits for them, and re-layouts: 0.43 us -> 2.61 us
    ppermute x5 -> x21, starting transfers between devices: 6.25 us -> 43.9 us  [the longest x3 8.95 us: local(): got = lax.ppermute(colsq, T, s)]
    all_to_all x2 -> x0, blocking collectives: 32.3 us -> none  [the longest x1 17.1 us: local(): rows = jnp.sum(lax.all_to_all(part.reshape(8, 32, RANK), T, 0, 0), axis=0)]
    ppermute x6, waiting for transfers between devices: 28.5 us -> 4.47 us  [ring_sum(): one, two, three = [lax.ppermute(v, F, s) for s in shifts]]
    ppermute x5 -> x21, waiting for transfers between devices: 7.23 us -> 21 us  [the longest x3 7.07 us: local(): us = [us[0]] + [lax.ppermute(us[k], F, YS[k - 1]) for k in (1, 2, 3)]]
    all_to_all x1 -> x0, starting transfers between devices: 6.76 us -> none  [local(): lax.all_to_all(u.reshape(16, 208, HALF), F, 0, 0, axis_index_groups=PLANE)]
    ppermute x1, starting transfers between devices: 0.03 us -> 3.65 us  [local(): u = join(u, lax.ppermute(u, F, CORE))]
    convert_element_type x3 -> x2, other arithmetic: 5.37 us -> 2.77 us  [the longest x1 1.58 us: local(): summed_b = (m2.astype(f32) + g2.astype(f32)).astype(bf16)]
    unnamed x10 -> x16, local copies, waits for them, and re-layouts: 0.29 us -> 2.47 us
  transfers between devices with their start and end apart: 15 -> 30, of which waited for: 11 -> 12; matrix products, arithmetic and copies ran while one was open for 6% -> 6% of each run, Pallas kernels for 27% -> 29%
where the time goes in v2:
time: 174 us
  starting transfers between devices  57.3 us (33%)
  Pallas kernels  51.2 us (29%)
  waiting for transfers between devices  25.5 us (15%)
  blocking collectives  17.6 us (10%)
  matrix products  11.9 us (7%)
  other arithmetic  7.02 us (4%)
  local copies, waits for them, and re-layouts  2.61 us (2%)
    pallas_call x1, Pallas kernels, inverse_factor(): pl.pallas_call(inverse_kernel, out_shape=jax.ShapeDtypeStruct((RANK, RANK...  49.4 us
    all_to_all x1, blocking collectives, local(): lax.all_to_all(jnp.broadcast_to(right, (16, 208, HALF)), F, 0, 0, axis_in...  17.6 us
    ppermute x3, starting transfers between devices, local(): got = lax.ppermute(colsq, T, s)  8.95 us
    ppermute x6, starting transfers between devices, ring_sum(): one, two, three = [lax.ppermute(v, F, s) for s in shifts]  7.85 us
    ppermute x3, waiting for transfers between devices, local(): us = [us[0]] + [lax.ppermute(us[k], F, YS[k - 1]) for k in (1, 2, 3)]  7.07 us
    ppermute x4, starting transfers between devices, local(): others = [lax.ppermute(p, F, CORE) for p in pieces]  6.24 us
    ppermute x2, waiting for transfers between devices, sum_over_z(): next_ = lambda v: lax.ppermute(v, T, ZS[1])  4.87 us
    ppermute x6, waiting for transfers between devices, ring_sum(): one, two, three = [lax.ppermute(v, F, s) for s in shifts]  4.47 us
  transfers between devices with their start and end apart: 30, of which 12 were waited for; matrix products, arithmetic and copies ran while one was open for 6% of the time, Pallas kernels for 29%

profile of v2, /device:TPU:33, one launch (start us, length us, event | category | flops | bytes accessed | tf_op | source)
XLA Modules:
  0.0 174.0 jit_solution(14860756826906238199)
XLA Ops:
  2.1 2.7 %fusion.5 = f32[256,256]{1,0:T(8,128)S(1)} fusion(bf16[3328,256]{1,0:T(8,128)(2,1)S(1)} %copy-done, bf16[256,3328]{1,0:T(8,128)(2,1)} %param.5, bf16[256,3328]{1,0:T(8,128)(2,1)} %param.4), kind=kOutput, calls=%fused_computation.11 | convolution fusion | flops 439615488 | bytes 5373952 | tf_op jit(solution)/shard_map/dot_general | solution.py:189
  4.8 1.6 add_convert_fusion
  7.0 1.7 collective-permute-start
  8.7 3.8 %collective-permute-done = f32[128,256]{1,0:T(8,128)S(1)} collective-permute-done((f32[128,256]{1,0:T(8,128)S(1)}, f32[128,256]{1,0:T(8,128)S(1)}, u32[]{:S(2)}, u32[]{:S(2)}) %collective-permute-start) | collective-permute-done | bytes 131104 | tf_op jit(solution)/shard_map/ppermute | solution.py:163
  12.5 2.9 %collective-permute-start.1 = (f32[64,256]{1,0:T(8,128)S(1)}, f32[64,256]{1,0:T(8,128)S(1)}, u32[]{:S(2)}, u32[]{:S(2)}) collective-permute-start(f32[64,256]{1,0:T(8,128)S(1)} %dynamic-slice_add_fusion.4), channel_id=1, source_target_pairs={{0,2},{1,3},{2,0},{3,1},{4,6},{5,7},{6,4},{7,5},{8,10},{9,11},{10,... | collective-permute-start | bytes 196616 | tf_op jit(solution)/shard_map/ppermute | solution.py:164
  15.3 2.5 %collective-permute-done.1 = f32[64,256]{1,0:T(8,128)S(1)} collective-permute-done((f32[64,256]{1,0:T(8,128)S(1)}, f32[64,256]{1,0:T(8,128)S(1)}, u32[]{:S(2)}, u32[]{:S(2)}) %collective-permute-start.1) | collective-permute-done | bytes 65568 | tf_op jit(solution)/shard_map/ppermute | solution.py:164
  17.9 4.2 %collective-permute-start.2 = (f32[64,256]{1,0:T(8,128)S(1)}, f32[64,256]{1,0:T(8,128)S(1)}, u32[]{:S(2)}, u32[]{:S(2)}) collective-permute-start(f32[64,256]{1,0:T(8,128)S(1)} %add_add_fusion.6), channel_id=1, source_target_pairs={{0,7},{1,6},{2,5},{3,4},{4,3},{5,2},{6,1},{7,0},{8,15},{9,14},{10,... | collective-permute-start | bytes 196616 | tf_op jit(solution)/shard_map/ppermute | solution.py:170
  22.1 2.0 %collective-permute-done.2 = f32[64,256]{1,0:T(8,128)S(1)} collective-permute-done((f32[64,256]{1,0:T(8,128)S(1)}, f32[64,256]{1,0:T(8,128)S(1)}, u32[]{:S(2)}, u32[]{:S(2)}) %collective-permute-start.2) | collective-permute-done | bytes 65568 | tf_op jit(solution)/shard_map/ppermute | solution.py:170
  26.0 2.3 %collective-permute-done.3.refs_1_ = f32[64,256]{1,0:T(8,128)S(1)} collective-permute-done((f32[64,256]{1,0:T(8,128)S(1)}, f32[64,256]{1,0:T(8,128)S(1)}, u32[]{:S(2)}, u32[]{:S(2)}) %collective-permute-start.3) | collective-permute-done | bytes 65568 | tf_op jit(solution)/shard_map/ppermute | solution.py:164
  28.4 1.5 collective-permute-start.5
  29.9 3.9 %collective-permute-start.6 = (f32[64,256]{1,0:T(8,128)S(1)}, f32[64,256]{1,0:T(8,128)S(1)}, u32[]{:S(2)}, u32[]{:S(2)}) collective-permute-start(f32[64,256]{1,0:T(8,128)S(1)} %add.269.refs_0_), channel_id=1, source_target_pairs={{0,8},{8,0},{16,24},{24,16},{32,40},{40,32},{48,56},{56,48},{64,72... | collective-permute-start | bytes 196616 | tf_op jit(solution)/shard_map/ppermute | solution.py:194
  34.4 1.8 %collective-permute-start.9 = (f32[64,256]{1,0:T(8,128)S(1)}, f32[64,256]{1,0:T(8,128)S(1)}, u32[]{:S(2)}, u32[]{:S(2)}) collective-permute-start(f32[64,256]{1,0:T(8,128)S(1)} %collective-permute-done.5.refs_3_), channel_id=1, source_target_pairs={{0,8},{8,0},{16,24},{24,16},{32,40},{40,32},{48,56},{56,48},{64,72... | collective-permute-start | bytes 196616 | tf_op jit(solution)/shard_map/ppermute | solution.py:194
  37.1 1.8 %assemble.1 = (bf16[512,256]{1,0:T(8,128)(2,1)S(1)}, f32[128,256]{1,0:T(8,128)S(1)}, f32[256,256]{1,0:T(8,128)S(1)}) custom-call(s32[2]{0:T(128)S(1)} %pad_add_fusion.place_ref.core_ref, f32[64,256]{1,0:T(8,128)S(1)} %add.269.refs_0_, f32[64,256]{1,0:T(8,128)S(1)} %collective-permute-done.3.refs_1_, f32[64,256]{1,0:T(8,128)S(1)} %collective-permute-done.4.refs_2_, ...), custom_call_target="tpu_custom_call" | custom-call | flops 200000000 | bytes 1200000 | tf_op jit(solution)/shard_map/assemble/pallas_call | solution.py:143
  40.2 2.1 %fusion.13 = f32[3328,256]{1,0:T(8,128)S(1)} fusion(bf16[256,3328]{1,0:T(8,128)(2,1)} %collective-permute-done.13, bf16[512,256]{1,0:T(8,128)(2,1)S(1)} %get-tuple-element.17), kind=kOutput, calls=%fused_computation.27 | convolution fusion | flops 436207616 | bytes 5242880 | tf_op jit(solution)/shard_map/dot_general | solution.py:200
  42.3 2.2 %convolution_add_fusion = f32[3328,256]{1,0:T(8,128)S(1)} fusion(f32[3328,256]{1,0:T(8,128)S(1)} %fusion.13, bf16[256,3328]{1,0:T(8,128)(2,1)} %add_convert_fusion, bf16[512,256]{1,0:T(8,128)(2,1)S(1)} %get-tuple-element.17), kind=kOutput, calls=%fused_computation.4 | convolution fusion | flops 437059584 | bytes 8650752 | tf_op jit(solution)/shard_map/dot_general | solution.py:200
  44.7 2.8 %collective-permute-start.16 = (f32[832,128]{1,0:T(8,128)S(1)}, f32[832,128]{1,0:T(8,128)S(1)}, u32[]{:S(2)}, u32[]{:S(2)}) collective-permute-start(f32[832,128]{1,0:T(8,128)S(1)} %get-tuple-element.24), channel_id=1, source_target_pairs={{0,48},{8,56},{16,0},{24,8},{32,16},{40,24},{48,32},{56,40},{64,11... | collective-permute-start | bytes 1277960 | tf_op jit(solution)/shard_map/ppermute | solution.py:211
  47.5 1.6 collective-permute-start.14
  50.7 1.5 collective-permute-start.10
  53.4 2.6 %collective-permute-done.10 = f32[128,256]{1,0:T(8,128)S(1)} collective-permute-done((f32[128,256]{1,0:T(8,128)S(1)}, f32[128,256]{1,0:T(8,128)S(1)}, u32[]{:S(2)}, u32[]{:S(2)}) %collective-permute-start.10) | collective-permute-done | bytes 131104 | tf_op jit(solution)/shard_map/ppermute | solution.py:37
  56.0 1.7 collective-permute-start.22
  60.4 7.1 %collective-permute-done.14 = f32[832,128]{1,0:T(8,128)} collective-permute-done((f32[832,128]{1,0:T(8,128)S(1)}, f32[832,128]{1,0:T(8,128)}, u32[]{:S(2)}, u32[]{:S(2)}) %collective-permute-start.14) | collective-permute-done | bytes 426016 | tf_op jit(solution)/shard_map/ppermute | solution.py:211
  72.2 2.5 %collective-permute-start.17 = (f32[208,128]{1,0:T(8,128)S(1)}, f32[208,128]{1,0:T(8,128)S(1)}, u32[]{:S(2)}, u32[]{:S(2)}) collective-permute-start(f32[208,128]{1,0:T(8,128)S(1)} %get-tuple-element.27), channel_id=1, source_target_pairs={{0,128},{8,136},{16,144},{24,152},{32,160},{40,168},{48,176},{56,1... | collective-permute-start | bytes 319496 | tf_op jit(solution)/shard_map/ppermute | solution.py:219
  75.7 4.3 %collective-permute-start.24 = (f32[128,256]{1,0:T(8,128)S(1)}, f32[128,256]{1,0:T(8,128)S(1)}, u32[]{:S(2)}, u32[]{:S(2)}) collective-permute-start(f32[128,256]{1,0:T(8,128)S(1)} %add_add_fusion.own_ref), channel_id=1, source_target_pairs={{0,8},{8,0},{16,24},{24,16},{32,40},{40,32},{48,56},{56,48},{64,72... | collective-permute-start | bytes 393224 | tf_op jit(solution)/shard_map/ppermute | solution.py:221
  81.0 3.6 %collective-permute-start.20 = (f32[208,128]{1,0:T(8,128)S(1)}, f32[208,128]{1,0:T(8,128)S(1)}, u32[]{:S(2)}, u32[]{:S(2)}) collective-permute-start(f32[208,128]{1,0:T(8,128)S(1)} %add_add_fusion.2), channel_id=1, source_target_pairs={{0,8},{8,0},{16,24},{24,16},{32,40},{40,32},{48,56},{56,48},{64,72... | collective-permute-start | bytes 319496 | tf_op jit(solution)/shard_map/ppermute | solution.py:222
  84.6 49.4 %inverse_factor.1 = f32[256,256]{1,0:T(8,128)S(1)} custom-call(s32[2]{0:T(128)S(1)} %pad_add_fusion.place_ref.core_ref, f32[128,256]{1,0:T(8,128)S(1)} %add_add_fusion.own_ref, f32[128,256]{1,0:T(8,128)S(1)} %collective-permute-done.24.other_ref), custom_call_target="tpu_custom_call" | custom-call | flops 5000000000 | bytes 600000 | tf_op jit(solution)/shard_map/inverse_factor/pallas_call | solution.py:103
  134.7 17.6 %all_to_all.5 = bf16[16,208,128]{2,1,0:T(8,128)(2,1)S(1)} all-to-all(bf16[16,208,128]{2,1,0:T(8,128)(2,1)S(1)} %broadcast_in_dim.6), channel_id=1, replica_groups={{0,64,128,192,16,80,144,208,32,96,160,224,48,112,176,240},{8,72,136,200..., dimensions={0} | all-to-all | bytes 1703936 | tf_op jit(solution)/shard_map/all_to_all | solution.py:228
  154.0 1.8 %collective-permute-start.25 = (f32[1,128]{1,0:T(1,128)S(1)}, f32[1,128]{1,0:T(1,128)S(1)}, u32[]{:S(2)}, u32[]{:S(2)}) collective-permute-start(f32[1,128]{1,0:T(1,128)S(1)} %bitcast.19), channel_id=1, source_target_pairs={{0,1},{1,0},{2,3},{3,2},{4,5},{5,4},{6,7},{7,6},{8,9},{9,8},{10,11... | collective-permute-start | bytes 1544 | tf_op jit(solution)/shard_map/ppermute | solution.py:236
  156.8 2.2 %collective-permute-start.26 = (f32[1,128]{1,0:T(1,128)S(1)}, f32[1,128]{1,0:T(1,128)S(1)}, u32[]{:S(2)}, u32[]{:S(2)}) collective-permute-start(f32[1,128]{1,0:T(1,128)S(1)} %bitcast_add_fusion), channel_id=1, source_target_pairs={{0,2},{1,3},{2,0},{3,1},{4,6},{5,7},{6,4},{7,5},{8,10},{9,11},{10,... | collective-permute-start | bytes 1544 | tf_op jit(solution)/shard_map/ppermute | solution.py:236
  160.0 5.0 %collective-permute-start.27 = (f32[1,128]{1,0:T(1,128)S(1)}, f32[1,128]{1,0:T(1,128)S(1)}, u32[]{:S(2)}, u32[]{:S(2)}) collective-permute-start(f32[1,128]{1,0:T(1,128)S(1)} %add.322), channel_id=1, source_target_pairs={{0,7},{1,6},{2,5},{3,4},{4,3},{5,2},{6,1},{7,0},{8,15},{9,14},{10,... | collective-permute-start | bytes 1544 | tf_op jit(solution)/shard_map/ppermute | solution.py:236
  165.0 2.3 %fusion.2 = bf16[256,3328]{1,0:T(8,128)(2,1)} fusion(bf16[256,256]{1,0:T(8,128)(2,1)S(1)} %convolution_convert_fusion, bf16[256,3328]{1,0:T(8,128)(2,1)S(1)} %copy-done.2, bf16[256,3328]{1,0:T(8,128)(2,1)S(1)} %copy-done.4, bf16[3328,128]{1,0:T(8,128)(2,1)S(1)} %collective-permute-done.28, bf16[3328,128]{1,0:T(8,128)(2,1)S(1)} %bitcast.17, pred[]{:T(512)S(6)} %eq.29), kind=kOutput, calls=%fused_computation.5 | convolution fusion | flops 448987136 | bytes 6946817 | tf_op jit(solution)/shard_map/dot_general | solution.py:232
  167.3 2.6 %collective-permute-start.29 = (f32[1,128]{1,0:T(1,128)S(1)}, f32[1,128]{1,0:T(1,128)S(1)}, u32[]{:S(2)}, u32[]{:S(2)}) collective-permute-start(f32[1,128]{1,0:T(1,128)S(1)} %add.323), channel_id=1, source_target_pairs={{0,8},{8,0},{16,24},{24,16},{32,40},{40,32},{48,56},{56,48},{64,72... | collective-permute-start | bytes 1544 | tf_op jit(solution)/shard_map/ppermute | solution.py:240
  172.2 1.8 %fusion.3 = bf16[256,3328]{1,0:T(8,128)(2,1)} fusion(bf16[256,256]{1,0:T(8,128)(2,1)S(1)} %convolution_convert_fusion, bf16[3328,256]{1,0:T(8,128)(2,1)S(1)} %multiply_convert_fusion, bf16[256,3328]{1,0:T(8,128)(2,1)S(1)} %copy-done.6), kind=kOutput, calls=%fused_computation.6 | convolution fusion | flops 439615488 | bytes 5242880 | tf_op jit(solution)/shard_map/dot_general | solution.py:242
  (73 shorter events, 25.8 us)
Async XLA Ops:
  6.3 33.8 %collective-permute-start.13 = (bf16[256,3328]{1,0:T(8,128)(2,1)}, bf16[256,3328]{1,0:T(8,128)(2,1)}, u32[]{:S(2)}, u32[]{:S(2)}) collective-permute-start(bf16[256,3328]{1,0:T(8,128)(2,1)} %add_convert_fusion), channel_id=1, source_target_pairs={{0,8},{8,0},{16,24},{24,16},{32,40},{40,32},{48,56},{56,48},{64,72... | collective-permute-start | bytes 5111816 | tf_op jit(solution)/shard_map/ppermute | solution.py:192
  7.0 5.4 %collective-permute-start = (f32[128,256]{1,0:T(8,128)S(1)}, f32[128,256]{1,0:T(8,128)S(1)}, u32[]{:S(2)}, u32[]{:S(2)}) collective-permute-start(f32[128,256]{1,0:T(8,128)S(1)} %constant_dynamic-slice_fusion), channel_id=1, source_target_pairs={{0,1},{1,0},{2,3},{3,2},{4,5},{5,4},{6,7},{7,6},{8,9},{9,8},{10,11... | collective-permute-start | bytes 393224 | tf_op jit(solution)/shard_map/ppermute | solution.py:163
  12.5 5.4 %collective-permute-start.1 = (f32[64,256]{1,0:T(8,128)S(1)}, f32[64,256]{1,0:T(8,128)S(1)}, u32[]{:S(2)}, u32[]{:S(2)}) collective-permute-start(f32[64,256]{1,0:T(8,128)S(1)} %dynamic-slice_add_fusion.4), channel_id=1, source_target_pairs={{0,2},{1,3},{2,0},{3,1},{4,6},{5,7},{6,4},{7,5},{8,10},{9,11},{10,... | collective-permute-start | bytes 196616 | tf_op jit(solution)/shard_map/ppermute | solution.py:164
  17.9 6.3 %collective-permute-start.2 = (f32[64,256]{1,0:T(8,128)S(1)}, f32[64,256]{1,0:T(8,128)S(1)}, u32[]{:S(2)}, u32[]{:S(2)}) collective-permute-start(f32[64,256]{1,0:T(8,128)S(1)} %add_add_fusion.6), channel_id=1, source_target_pairs={{0,7},{1,6},{2,5},{3,4},{4,3},{5,2},{6,1},{7,0},{8,15},{9,14},{10,... | collective-permute-start | bytes 196616 | tf_op jit(solution)/shard_map/ppermute | solution.py:170
  24.2 4.2 %collective-permute-start.3 = (f32[64,256]{1,0:T(8,128)S(1)}, f32[64,256]{1,0:T(8,128)S(1)}, u32[]{:S(2)}, u32[]{:S(2)}) collective-permute-start(f32[64,256]{1,0:T(8,128)S(1)} %add.269.refs_0_), channel_id=1, source_target_pairs={{0,2},{1,3},{2,0},{3,1},{4,6},{5,7},{6,4},{7,5},{8,10},{9,11},{10,... | collective-permute-start | bytes 196616 | tf_op jit(solution)/shard_map/ppermute | solution.py:164
  25.6 8.2 %collective-permute-start.4 = (f32[64,256]{1,0:T(8,128)S(1)}, f32[64,256]{1,0:T(8,128)S(1)}, u32[]{:S(2)}, u32[]{:S(2)}) collective-permute-start(f32[64,256]{1,0:T(8,128)S(1)} %add.269.refs_0_), channel_id=1, source_target_pairs={{0,1},{1,0},{2,3},{3,2},{4,5},{5,4},{6,7},{7,6},{8,9},{9,8},{10,11... | collective-permute-start | bytes 196616 | tf_op jit(solution)/shard_map/ppermute | solution.py:163
  28.4 6.0 %collective-permute-start.5 = (f32[64,256]{1,0:T(8,128)S(1)}, f32[64,256]{1,0:T(8,128)S(1)}, u32[]{:S(2)}, u32[]{:S(2)}) collective-permute-start(f32[64,256]{1,0:T(8,128)S(1)} %collective-permute-done.3.refs_1_), channel_id=1, source_target_pairs={{0,1},{1,0},{2,3},{3,2},{4,5},{5,4},{6,7},{7,6},{8,9},{9,8},{10,11... | collective-permute-start | bytes 196616 | tf_op jit(solution)/shard_map/ppermute | solution.py:163
  29.9 6.3 %collective-permute-start.6 = (f32[64,256]{1,0:T(8,128)S(1)}, f32[64,256]{1,0:T(8,128)S(1)}, u32[]{:S(2)}, u32[]{:S(2)}) collective-permute-start(f32[64,256]{1,0:T(8,128)S(1)} %add.269.refs_0_), channel_id=1, source_target_pairs={{0,8},{8,0},{16,24},{24,16},{32,40},{40,32},{48,56},{56,48},{64,72... | collective-permute-start | bytes 196616 | tf_op jit(solution)/shard_map/ppermute | solution.py:194
  33.8 2.4 %collective-permute-start.7 = (f32[64,256]{1,0:T(8,128)S(1)}, f32[64,256]{1,0:T(8,128)S(1)}, u32[]{:S(2)}, u32[]{:S(2)}) collective-permute-start(f32[64,256]{1,0:T(8,128)S(1)} %collective-permute-done.3.refs_1_), channel_id=1, source_target_pairs={{0,8},{8,0},{16,24},{24,16},{32,40},{40,32},{48,56},{56,48},{64,72... | collective-permute-start | bytes 196616 | tf_op jit(solution)/shard_map/ppermute | solution.py:194
  33.8 2.4 %collective-permute-start.8 = (f32[64,256]{1,0:T(8,128)S(1)}, f32[64,256]{1,0:T(8,128)S(1)}, u32[]{:S(2)}, u32[]{:S(2)}) collective-permute-start(f32[64,256]{1,0:T(8,128)S(1)} %collective-permute-done.4.refs_2_), channel_id=1, source_target_pairs={{0,8},{8,0},{16,24},{24,16},{32,40},{40,32},{48,56},{56,48},{64,72... | collective-permute-start | bytes 196616 | tf_op jit(solution)/shard_map/ppermute | solution.py:194
  34.4 2.7 %collective-permute-start.9 = (f32[64,256]{1,0:T(8,128)S(1)}, f32[64,256]{1,0:T(8,128)S(1)}, u32[]{:S(2)}, u32[]{:S(2)}) collective-permute-start(f32[64,256]{1,0:T(8,128)S(1)} %collective-permute-done.5.refs_3_), channel_id=1, source_target_pairs={{0,8},{8,0},{16,24},{24,16},{32,40},{40,32},{48,56},{56,48},{64,72... | collective-permute-start | bytes 196616 | tf_op jit(solution)/shard_map/ppermute | solution.py:194
  38.9 11.8 %collective-permute-start.11 = (f32[128,256]{1,0:T(8,128)S(1)}, f32[128,256]{1,0:T(8,128)S(1)}, u32[]{:S(2)}, u32[]{:S(2)}) collective-permute-start(f32[128,256]{1,0:T(8,128)S(1)} %get-tuple-element.14), channel_id=1, source_target_pairs={{0,64},{8,72},{16,80},{24,88},{32,96},{40,104},{48,112},{56,120},{... | collective-permute-start | bytes 393224 | tf_op jit(solution)/shard_map/ppermute | solution.py:37
  44.7 14.0 %collective-permute-start.16 = (f32[832,128]{1,0:T(8,128)S(1)}, f32[832,128]{1,0:T(8,128)S(1)}, u32[]{:S(2)}, u32[]{:S(2)}) collective-permute-start(f32[832,128]{1,0:T(8,128)S(1)} %get-tuple-element.24), channel_id=1, source_target_pairs={{0,48},{8,56},{16,0},{24,8},{32,16},{40,24},{48,32},{56,40},{64,11... | collective-permute-start | bytes 1277960 | tf_op jit(solution)/shard_map/ppermute | solution.py:211
  47.5 12.8 %collective-permute-start.15 = (f32[832,128]{1,0:T(8,128)S(1)}, f32[832,128]{1,0:T(8,128)}, u32[]{:S(2)}, u32[]{:S(2)}) collective-permute-start(f32[832,128]{1,0:T(8,128)S(1)} %get-tuple-element.25), channel_id=1, source_target_pairs={{0,16},{8,24},{16,32},{24,40},{32,48},{40,56},{48,0},{56,8},{64,80... | collective-permute-start | bytes 1277960 | tf_op jit(solution)/shard_map/ppermute | solution.py:211
  47.5 19.9 %collective-permute-start.14 = (f32[832,128]{1,0:T(8,128)S(1)}, f32[832,128]{1,0:T(8,128)}, u32[]{:S(2)}, u32[]{:S(2)}) collective-permute-start(f32[832,128]{1,0:T(8,128)S(1)} %get-tuple-element.23), channel_id=1, source_target_pairs={{0,32},{8,40},{16,48},{24,56},{32,0},{40,8},{48,16},{56,24},{64,96... | collective-permute-start | bytes 1277960 | tf_op jit(solution)/shard_map/ppermute | solution.py:211
  49.2 4.2 %collective-permute-start.12 = (f32[128,256]{1,0:T(8,128)S(1)}, f32[128,256]{1,0:T(8,128)S(1)}, u32[]{:S(2)}, u32[]{:S(2)}) collective-permute-start(f32[128,256]{1,0:T(8,128)S(1)} %get-tuple-element.14), channel_id=1, source_target_pairs={{0,192},{8,200},{16,208},{24,216},{32,224},{40,232},{48,240},{56,2... | collective-permute-start | bytes 393224 | tf_op jit(solution)/shard_map/ppermute | solution.py:37
  50.7 5.3 %collective-permute-start.10 = (f32[128,256]{1,0:T(8,128)S(1)}, f32[128,256]{1,0:T(8,128)S(1)}, u32[]{:S(2)}, u32[]{:S(2)}) collective-permute-start(f32[128,256]{1,0:T(8,128)S(1)} %get-tuple-element.14), channel_id=1, source_target_pairs={{0,128},{8,136},{16,144},{24,152},{32,160},{40,168},{48,176},{56,1... | collective-permute-start | bytes 393224 | tf_op jit(solution)/shard_map/ppermute | solution.py:37
  56.0 16.2 %collective-permute-start.22 = (f32[128,256]{1,0:T(8,128)S(1)}, f32[128,256]{1,0:T(8,128)S(1)}, u32[]{:S(2)}, u32[]{:S(2)}) collective-permute-start(f32[128,256]{1,0:T(8,128)S(1)} %add_add_fusion.1), channel_id=1, source_target_pairs={{0,16},{8,24},{16,32},{24,40},{32,48},{40,56},{48,0},{56,8},{64,80... | collective-permute-start | bytes 393224 | tf_op jit(solution)/shard_map/ppermute | solution.py:37
  57.7 16.9 %collective-permute-start.23 = (f32[128,256]{1,0:T(8,128)S(1)}, f32[128,256]{1,0:T(8,128)}, u32[]{:S(2)}, u32[]{:S(2)}) collective-permute-start(f32[128,256]{1,0:T(8,128)S(1)} %add_add_fusion.1), channel_id=1, source_target_pairs={{0,48},{8,56},{16,0},{24,8},{32,16},{40,24},{48,32},{56,40},{64,11... | collective-permute-start | bytes 393224 | tf_op jit(solution)/shard_map/ppermute | solution.py:37
  59.5 15.1 %collective-permute-start.21 = (f32[128,256]{1,0:T(8,128)S(1)}, f32[128,256]{1,0:T(8,128)}, u32[]{:S(2)}, u32[]{:S(2)}) collective-permute-start(f32[128,256]{1,0:T(8,128)S(1)} %add_add_fusion.1), channel_id=1, source_target_pairs={{0,32},{8,40},{16,48},{24,56},{32,0},{40,8},{48,16},{56,24},{64,96... | collective-permute-start | bytes 393224 | tf_op jit(solution)/shard_map/ppermute | solution.py:37
  68.8 11.2 %collective-permute-start.18 = (f32[208,128]{1,0:T(8,128)S(1)}, f32[208,128]{1,0:T(8,128)S(1)}, u32[]{:S(2)}, u32[]{:S(2)}) collective-permute-start(f32[208,128]{1,0:T(8,128)S(1)} %get-tuple-element.29), channel_id=1, source_target_pairs={{0,64},{8,72},{16,80},{24,88},{32,96},{40,104},{48,112},{56,120},{... | collective-permute-start | bytes 319496 | tf_op jit(solution)/shard_map/ppermute | solution.py:220
  70.0 9.9 %collective-permute-start.19 = (f32[208,128]{1,0:T(8,128)S(1)}, f32[208,128]{1,0:T(8,128)S(1)}, u32[]{:S(2)}, u32[]{:S(2)}) collective-permute-start(f32[208,128]{1,0:T(8,128)S(1)} %get-tuple-element.28), channel_id=1, source_target_pairs={{0,192},{8,200},{16,208},{24,216},{32,224},{40,232},{48,240},{56,2... | collective-permute-start | bytes 319496 | tf_op jit(solution)/shard_map/ppermute | solution.py:220
  72.2 7.7 %collective-permute-start.17 = (f32[208,128]{1,0:T(8,128)S(1)}, f32[208,128]{1,0:T(8,128)S(1)}, u32[]{:S(2)}, u32[]{:S(2)}) collective-permute-start(f32[208,128]{1,0:T(8,128)S(1)} %get-tuple-element.27), channel_id=1, source_target_pairs={{0,128},{8,136},{16,144},{24,152},{32,160},{40,168},{48,176},{56,1... | collective-permute-start | bytes 319496 | tf_op jit(solution)/shard_map/ppermute | solution.py:219
  75.7 9.0 %collective-permute-start.24 = (f32[128,256]{1,0:T(8,128)S(1)}, f32[128,256]{1,0:T(8,128)S(1)}, u32[]{:S(2)}, u32[]{:S(2)}) collective-permute-start(f32[128,256]{1,0:T(8,128)S(1)} %add_add_fusion.own_ref), channel_id=1, source_target_pairs={{0,8},{8,0},{16,24},{24,16},{32,40},{40,32},{48,56},{56,48},{64,72... | collective-permute-start | bytes 393224 | tf_op jit(solution)/shard_map/ppermute | solution.py:221
  81.0 53.1 %collective-permute-start.20 = (f32[208,128]{1,0:T(8,128)S(1)}, f32[208,128]{1,0:T(8,128)S(1)}, u32[]{:S(2)}, u32[]{:S(2)}) collective-permute-start(f32[208,128]{1,0:T(8,128)S(1)} %add_add_fusion.2), channel_id=1, source_target_pairs={{0,8},{8,0},{16,24},{24,16},{32,40},{40,32},{48,56},{56,48},{64,72... | collective-permute-start | bytes 319496 | tf_op jit(solution)/shard_map/ppermute | solution.py:222
  134.5 30.5 %copy-start.4 = (bf16[256,3328]{1,0:T(8,128)(2,1)S(1)}, bf16[256,3328]{1,0:T(8,128)(2,1)}, u32[]{:S(2)}) copy-start(bf16[256,3328]{1,0:T(8,128)(2,1)} %param.4) | copy-start | bytes 5111812
  134.7 30.4 %copy-start.2 = (bf16[256,3328]{1,0:T(8,128)(2,1)S(1)}, bf16[256,3328]{1,0:T(8,128)(2,1)}, u32[]{:S(2)}) copy-start(bf16[256,3328]{1,0:T(8,128)(2,1)} %param.5) | copy-start | bytes 5111812
  152.3 12.7 %collective-permute-start.28 = (bf16[3328,128]{1,0:T(8,128)(2,1)S(1)}, bf16[3328,128]{1,0:T(8,128)(2,1)S(1)}, u32[]{:S(2)}, u32[]{:S(2)}) collective-permute-start(bf16[3328,128]{1,0:T(8,128)(2,1)S(1)} %bitcast.16), channel_id=1, source_target_pairs={{0,8},{8,0},{16,24},{24,16},{32,40},{40,32},{48,56},{56,48},{64,72... | collective-permute-start | bytes 2555912 | tf_op jit(solution)/shard_map/ppermute | solution.py:231
  154.0 2.8 %collective-permute-start.25 = (f32[1,128]{1,0:T(1,128)S(1)}, f32[1,128]{1,0:T(1,128)S(1)}, u32[]{:S(2)}, u32[]{:S(2)}) collective-permute-start(f32[1,128]{1,0:T(1,128)S(1)} %bitcast.19), channel_id=1, source_target_pairs={{0,1},{1,0},{2,3},{3,2},{4,5},{5,4},{6,7},{7,6},{8,9},{9,8},{10,11... | collective-permute-start | bytes 1544 | tf_op jit(solution)/shard_map/ppermute | solution.py:236
  156.8 3.3 %collective-permute-start.26 = (f32[1,128]{1,0:T(1,128)S(1)}, f32[1,128]{1,0:T(1,128)S(1)}, u32[]{:S(2)}, u32[]{:S(2)}) collective-permute-start(f32[1,128]{1,0:T(1,128)S(1)} %bitcast_add_fusion), channel_id=1, source_target_pairs={{0,2},{1,3},{2,0},{3,1},{4,6},{5,7},{6,4},{7,5},{8,10},{9,11},{10,... | collective-permute-start | bytes 1544 | tf_op jit(solution)/shard_map/ppermute | solution.py:236
  160.0 7.2 %collective-permute-start.27 = (f32[1,128]{1,0:T(1,128)S(1)}, f32[1,128]{1,0:T(1,128)S(1)}, u32[]{:S(2)}, u32[]{:S(2)}) collective-permute-start(f32[1,128]{1,0:T(1,128)S(1)} %add.322), channel_id=1, source_target_pairs={{0,7},{1,6},{2,5},{3,4},{4,3},{5,2},{6,1},{7,0},{8,15},{9,14},{10,... | collective-permute-start | bytes 1544 | tf_op jit(solution)/shard_map/ppermute | solution.py:236
  167.3 3.4 %collective-permute-start.29 = (f32[1,128]{1,0:T(1,128)S(1)}, f32[1,128]{1,0:T(1,128)S(1)}, u32[]{:S(2)}, u32[]{:S(2)}) collective-permute-start(f32[1,128]{1,0:T(1,128)S(1)} %add.323), channel_id=1, source_target_pairs={{0,8},{8,0},{16,24},{24,16},{32,40},{40,32},{48,56},{56,48},{64,72... | collective-permute-start | bytes 1544 | tf_op jit(solution)/shard_map/ppermute | solution.py:240
  (6 other events, 13.7 us)

commit v3 on v2

--- a/solution.py
+++ b/solution.py
@@ -112,48 +112,103 @@
     )(core, own, other)
 
 
-def assemble_kernel(place_ref, *refs):
-    pieces, (split_ref, gram_ref, proj_ref, other_ref, sems) = refs[:8], refs[8:]
-    first = place_ref[0] == 0
-    order = place_ref[1]
-    copies = []
-    for n, piece in enumerate(pieces):
-        at = pl.multiple_of(jnp.bitwise_xor(order, n % 4) * 64, 64)
-        target = (proj_ref if n < 4 else other_ref).at[pl.ds(at, 64), :]
-        copies.append(pltpu.make_async_copy(piece, target, sems.at[n]))
-    for copy in copies:
-        copy.start()
-    for copy in copies:
-        copy.wait()
-    grams = []
-    for at, ref in ((0, proj_ref), (256, other_ref)):
-        whole = ref[...]
-        mine = jnp.where(first, whole[:, :HALF], whole[:, HALF:])
-        high = mine.astype(bf16)
-        split_ref[at : at + 256, :HALF] = high
-        split_ref[at : at + 256, HALF:] = (mine - high.astype(f32)).astype(bf16)
-        grams.append(
-            lax.dot_general(mine, whole, (((0,), (0,)), ((), ())), precision=HIGH, preferred_element_type=f32)
-        )
-    gram_ref[...] = grams[0] + grams[1]
-
-
-def assemble(now, pieces):
-    vmem = pl.BlockSpec(memory_space=pltpu.VMEM)
+WIDE = 1664
+
+
+def project_kernel(m_ref, g_ref, basis_ref, s_ref, part_ref):
+    s = (m_ref[...].astype(f32) + g_ref[...].astype(f32)).astype(bf16)
+    s_ref[...] = s
+    part = jnp.dot(s, basis_ref[...], preferred_element_type=f32)
+
+    @pl.when(pl.program_id(0) == 0)
+    def _():
+        part_ref[...] = part
+
+    @pl.when(pl.program_id(0) > 0)
+    def _():
+        part_ref[...] += part
+
+
+def project(momentum, gradient, basis):
+    columns = pl.BlockSpec((256, WIDE), lambda i: (0, i))
     return pl.pallas_call(
-        assemble_kernel,
-        in_specs=[pl.BlockSpec(memory_space=pltpu.SMEM)] + [pl.BlockSpec(memory_space=pl.ANY)] * 8,
-        out_specs=[vmem] * 3,
+        project_kernel,
+        grid=(2,),
+        in_specs=[columns, columns, pl.BlockSpec((WIDE, RANK), lambda i: (i, 0))],
+        out_specs=[columns, pl.BlockSpec((256, RANK), lambda i: (0, 0))],
         out_shape=[
-            jax.ShapeDtypeStruct((512, RANK), bf16),
-            jax.ShapeDtypeStruct((HALF, RANK), f32),
+            jax.ShapeDtypeStruct((256, 3328), bf16),
             jax.ShapeDtypeStruct((256, RANK), f32),
         ],
-        scratch_shapes=[pltpu.VMEM((256, RANK), f32), pltpu.SemaphoreType.DMA((8,))],
-        compiler_params=pltpu.CompilerParams(vmem_limit_bytes=4 * 1024 * 1024),
-        cost_estimate=pl.CostEstimate(flops=200_000_000, bytes_accessed=1_200_000, transcendentals=0),
-        name="assemble",
-    )(now, *pieces)
+        compiler_params=pltpu.CompilerParams(vmem_limit_bytes=24 * 1024 * 1024),
+        cost_estimate=pl.CostEstimate(flops=440_000_000, bytes_accessed=7_000_000, transcendentals=0),
+        name="project",
+    )(momentum, gradient, basis)
+
+
+def spread_kernel(place_ref, s_ref, so_ref, *refs):
+    pieces, refs = refs[:8], refs[8:]
+    outs, (gram_ref, proj_ref, other_ref, split_ref, sems) = refs[:4], refs[4:]
+    step = pl.program_id(0)
+
+    @pl.when(step == 0)
+    def _():
+        first = place_ref[0] == 0
+        order = place_ref[1]
+        copies = []
+        for n, piece in enumerate(pieces):
+            at = pl.multiple_of(jnp.bitwise_xor(order, n % 4) * 64, 64)
+            target = (proj_ref if n < 4 else other_ref).at[pl.ds(at, 64), :]
+            copies.append(pltpu.make_async_copy(piece, target, sems.at[n]))
+        for copy in copies:
+            copy.start()
+        for copy in copies:
+            copy.wait()
+        grams = []
+        for at, ref in ((0, proj_ref), (256, other_ref)):
+            whole = ref[...]
+            mine = jnp.where(first, whole[:, :HALF], whole[:, HALF:])
+            turned = mine.T
+            high = turned.astype(bf16)
+            split_ref[:HALF, at : at + 256] = high
+            split_ref[HALF:, at : at + 256] = (turned - high.astype(f32)).astype(bf16)
+            grams.append(jnp.dot(turned, whole, precision=HIGH, preferred_element_type=f32))
+        gram_ref[...] = grams[0] + grams[1]
+
+    u = jnp.dot(split_ref[:, :256], s_ref[...], preferred_element_type=f32)
+    u = u + jnp.dot(split_ref[:, 256:], so_ref[...], preferred_element_type=f32)
+    u = (u[:HALF, :] + u[HALF:, :]).T
+    for j in range(2):
+        ahead = jnp.bitwise_and(step * 2 + j + 4 - place_ref[2], 3)
+        for k in range(4):
+
+            @pl.when(ahead == k)
+            def _():
+                outs[k][...] = u[j * 832 : (j + 1) * 832, :]
+
+
+def spread(now, summed_b, summed_o, pieces):
+    columns = pl.BlockSpec((256, WIDE), lambda i, p: (0, i))
+    whole = lambda *shape: pl.BlockSpec(shape, lambda i, p: (0, 0))
+    return pl.pallas_call(
+        spread_kernel,
+        grid_spec=pltpu.PrefetchScalarGridSpec(
+            num_scalar_prefetch=1,
+            grid=(2,),
+            in_specs=[columns, columns] + [pl.BlockSpec(memory_space=pl.ANY)] * 8,
+            out_specs=[whole(832, HALF)] * 4 + [whole(HALF, RANK), whole(256, RANK)],
+            scratch_shapes=[
+                pltpu.VMEM((256, RANK), f32),
+                pltpu.VMEM((RANK, 512), bf16),
+                pltpu.SemaphoreType.DMA((8,)),
+            ],
+        ),
+        out_shape=[jax.ShapeDtypeStruct((832, HALF), f32)] * 4
+        + [jax.ShapeDtypeStruct((HALF, RANK), f32), jax.ShapeDtypeStruct((256, RANK), f32)],
+        compiler_params=pltpu.CompilerParams(vmem_limit_bytes=32 * 1024 * 1024),
+        cost_estimate=pl.CostEstimate(flops=2_000_000_000, bytes_accessed=6_000_000, transcendentals=0),
+        name="spread",
+    )(now, summed_b, summed_o, *pieces)
 
 
 def sum_over_z(part):
@@ -185,29 +240,17 @@
         return lax.dynamic_slice_in_dim(v, core * HALF, HALF, axis=-1)
 
     summed = momentum.astype(f32) + gradient.astype(f32)
-    summed_b = summed.astype(bf16)
-    part = jnp.dot(summed_b, basis, preferred_element_type=f32)
-    part, m2, g2 = lax.optimization_barrier((part, momentum, gradient))
-    summed_b = (m2.astype(f32) + g2.astype(f32)).astype(bf16)
+    summed_b, part = project(momentum, gradient, basis)
     summed_o = lax.ppermute(summed_b, F, CORE)
     pieces, order = sum_over_z(part)
     others = [lax.ppermute(p, F, CORE) for p in pieces]
     place_x, place_y = lax.axis_index(F) // 8, lax.axis_index(F) // 2 % 4
-
-    now = jnp.stack([core, order]).astype(jnp.int32)
-    split, gram, proj = assemble(now, [*pieces, *others])
-    over_rows = (((0,), (0,)), ((), ()))
-    u = lax.dot_general(summed_b, split[:256], over_rows, preferred_element_type=f32) + lax.dot_general(
-        summed_o, split[256:], over_rows, preferred_element_type=f32
-    )
+    now = jnp.stack([core, order, place_y]).astype(jnp.int32)
+    *us, gram, proj = spread(now, summed_b, summed_o, [*pieces, *others])
 
     def along(v, k, here, size):
         return lax.dynamic_slice_in_dim(v, (here + k) % 4 * size, size, 0)
 
-    us = []
-    for k in range(4):
-        w = along(u, k, place_y, 832)
-        us.append(w[:, :HALF] + w[:, HALF:])
     us = [us[0]] + [lax.ppermute(us[k], F, YS[k - 1]) for k in (1, 2, 3)]
     gram = ring_sum(gram, XS)
     gram, us[0] = lax.optimization_barrier((gram, us[0]))

time: 174 us -> 170 us (0.977)
  matrix products: 11.9 us -> 4.94 us
  other arithmetic: 7.02 us -> 2.01 us
  starting transfers between devices: 57.3 us -> 52.9 us
  Pallas kernels: 51.2 us -> 55.4 us
  waiting for transfers between devices: 25.5 us -> 28.8 us
  local copies, waits for them, and re-layouts: 2.61 us -> 4.76 us
  blocking collectives: 17.6 us -> 19.6 us
    dot_general x3 -> x0, matrix products: 6.96 us -> none  [the longest x1 2.65 us: local(): part = jnp.dot(summed_b, basis, preferred_element_type=f32)]
    pallas_call x1 -> x2, Pallas kernels: 1.81 us -> 6.02 us  [the longest x1 4.74 us: spread(): pl.pallas_call(spread_kernel, grid_spec=pltpu.PrefetchScalarGridSpec(num_...]
    ppermute x1, starting transfers between devices: 4.26 us -> 0.97 us  [local(): inv = inverse_factor(now, gram, lax.ppermute(gram, F, CORE))]
    ppermute x2, waiting for transfers between devices: 0.01 us -> 2.62 us  [local(): u = u + (lax.ppermute(vs[1], F, XS[0]) + lax.ppermute(vs[3], F, XS[2]))]
    ppermute x1, starting transfers between devices: 3.65 us -> 1.1 us  [local(): u = join(u, lax.ppermute(u, F, CORE))]
    unnamed x16 -> x14, local copies, waits for them, and re-layouts: 2.47 us -> 4.63 us
    ppermute x1, starting transfers between devices: 2.45 us -> 0.32 us  [local(): u = vs[0] + lax.ppermute(vs[2], F, XS[1])]
    all_to_all x1, blocking collectives: 17.6 us -> 19.6 us  [local(): lax.all_to_all(jnp.broadcast_to(right, (16, 208, HALF)), F, 0, 0, axis_in...]
  transfers between devices with their start and end apart: 30 -> 30, of which waited for: 12 -> 13; matrix products, arithmetic and copies ran while one was open for 6% -> 2% of each run, Pallas kernels for 29% -> 29%
where the time goes in v3:
time: 170 us; the launch traced here: 169 us
  Pallas kernels  55.4 us (33%)
  starting transfers between devices  52.9 us (31%)
  waiting for transfers between devices  28.8 us (17%)
  blocking collectives  19.6 us (12%)
  matrix products  4.94 us (3%)
  local copies, waits for them, and re-layouts  4.76 us (3%)
  other arithmetic  2.01 us (1%)
    pallas_call x1, Pallas kernels, inverse_factor(): pl.pallas_call(inverse_kernel, out_shape=jax.ShapeDtypeStruct((RANK, RANK...  49.4 us
    all_to_all x1, blocking collectives, local(): lax.all_to_all(jnp.broadcast_to(right, (16, 208, HALF)), F, 0, 0, axis_in...  19.6 us
    ppermute x3, starting transfers between devices, local(): got = lax.ppermute(colsq, T, s)  9 us
    ppermute x3, waiting for transfers between devices, local(): us = [us[0]] + [lax.ppermute(us[k], F, YS[k - 1]) for k in (1, 2, 3)]  8.95 us
    ppermute x6, starting transfers between devices, ring_sum(): one, two, three = [lax.ppermute(v, F, s) for s in shifts]  8.91 us
    ppermute x4, starting transfers between devices, local(): others = [lax.ppermute(p, F, CORE) for p in pieces]  6.5 us
    ppermute x3, starting transfers between devices, local(): us = [us[0]] + [lax.ppermute(us[k], F, YS[k - 1]) for k in (1, 2, 3)]  5.59 us
    ppermute x1, starting transfers between devices, sum_over_z(): a = kept + lax.ppermute(kept, T, ZS[2])  5.02 us
  transfers between devices with their start and end apart: 30, of which 13 were waited for; matrix products, arithmetic and copies ran while one was open for 2% of the time, Pallas kernels for 29%

profile of v3, /device:TPU:33, one launch (start us, length us, event | category | flops | bytes accessed | tf_op | source)
XLA Modules:
  0.0 169.3 jit_solution(3855753167664031567)
XLA Ops:
  2.1 1.5 copy-done.1
  3.5 1.5 copy-done.3
  7.1 1.7 collective-permute-start.1
  8.7 3.7 %collective-permute-done.1 = f32[128,256]{1,0:T(8,128)S(1)} collective-permute-done((f32[128,256]{1,0:T(8,128)S(1)}, f32[128,256]{1,0:T(8,128)S(1)}, u32[]{:S(2)}, u32[]{:S(2)}) %collective-permute-start.1) | collective-permute-done | bytes 131104 | tf_op jit(solution)/shard_map/ppermute | solution.py:218
  12.5 2.9 %collective-permute-start.2 = (f32[64,256]{1,0:T(8,128)S(1)}, f32[64,256]{1,0:T(8,128)S(1)}, u32[]{:S(2)}, u32[]{:S(2)}) collective-permute-start(f32[64,256]{1,0:T(8,128)S(1)} %dynamic-slice_add_fusion), channel_id=1, source_target_pairs={{0,2},{1,3},{2,0},{3,1},{4,6},{5,7},{6,4},{7,5},{8,10},{9,11},{10,... | collective-permute-start | bytes 196616 | tf_op jit(solution)/shard_map/ppermute | solution.py:219
  15.3 1.8 %collective-permute-done.2 = f32[64,256]{1,0:T(8,128)S(1)} collective-permute-done((f32[64,256]{1,0:T(8,128)S(1)}, f32[64,256]{1,0:T(8,128)S(1)}, u32[]{:S(2)}, u32[]{:S(2)}) %collective-permute-start.2) | collective-permute-done | bytes 65568 | tf_op jit(solution)/shard_map/ppermute | solution.py:219
  17.1 5.0 %collective-permute-start.3 = (f32[64,256]{1,0:T(8,128)S(1)}, f32[64,256]{1,0:T(8,128)S(1)}, u32[]{:S(2)}, u32[]{:S(2)}) collective-permute-start(f32[64,256]{1,0:T(8,128)S(1)} %add_add_fusion.6), channel_id=1, source_target_pairs={{0,7},{1,6},{2,5},{3,4},{4,3},{5,2},{6,1},{7,0},{8,15},{9,14},{10,... | collective-permute-start | bytes 196616 | tf_op jit(solution)/shard_map/ppermute | solution.py:225
  22.1 1.9 %collective-permute-done.3 = f32[64,256]{1,0:T(8,128)S(1)} collective-permute-done((f32[64,256]{1,0:T(8,128)S(1)}, f32[64,256]{1,0:T(8,128)S(1)}, u32[]{:S(2)}, u32[]{:S(2)}) %collective-permute-start.3) | collective-permute-done | bytes 65568 | tf_op jit(solution)/shard_map/ppermute | solution.py:225
  24.0 1.5 collective-permute-start.4
  26.0 2.3 %collective-permute-done.4.refs_1_ = f32[64,256]{1,0:T(8,128)S(1)} collective-permute-done((f32[64,256]{1,0:T(8,128)S(1)}, f32[64,256]{1,0:T(8,128)S(1)}, u32[]{:S(2)}, u32[]{:S(2)}) %collective-permute-start.4) | collective-permute-done | bytes 65568 | tf_op jit(solution)/shard_map/ppermute | solution.py:219
  28.2 1.5 collective-permute-start.6
  29.8 4.2 %collective-permute-start.7 = (f32[64,256]{1,0:T(8,128)S(1)}, f32[64,256]{1,0:T(8,128)S(1)}, u32[]{:S(2)}, u32[]{:S(2)}) collective-permute-start(f32[64,256]{1,0:T(8,128)S(1)} %add.218.refs_0_), channel_id=1, source_target_pairs={{0,8},{8,0},{16,24},{24,16},{32,40},{40,32},{48,56},{56,48},{64,72... | collective-permute-start | bytes 196616 | tf_op jit(solution)/shard_map/ppermute | solution.py:246
  34.5 1.8 %collective-permute-start.10 = (f32[64,256]{1,0:T(8,128)S(1)}, f32[64,256]{1,0:T(8,128)S(1)}, u32[]{:S(2)}, u32[]{:S(2)}) collective-permute-start(f32[64,256]{1,0:T(8,128)S(1)} %collective-permute-done.6.refs_3_), channel_id=1, source_target_pairs={{0,8},{8,0},{16,24},{24,16},{32,40},{40,32},{48,56},{56,48},{64,72... | collective-permute-start | bytes 196616 | tf_op jit(solution)/shard_map/ppermute | solution.py:246
  37.2 4.7 %spread.1 = (f32[832,128]{1,0:T(8,128)S(1)}, f32[832,128]{1,0:T(8,128)S(1)}, f32[832,128]{1,0:T(8,128)S(1)}, f32[832,128]{1,0:T(8,128)S(1)}, f32[128,256]{1,0:T(8,128)S(1)}, /*index=5*/f32[256,256]{1,0:T(8,128)S(1)}) custom-call(s32[3]{0:T(128)S(1)} %pad_add_fusion.place_ref.core_ref, bf16[256,3328]{1,0:T(8,128)(2,1)S(1)} %get-tuple-element.15.s_ref, ...), custom_call_target="tpu_custom_call" | custom-call | flops 2000000000 | bytes 6000000 | tf_op jit(solution)/shard_map/spread/pallas_call | solution.py:193
  41.9 2.8 %collective-permute-start.11 = (f32[128,256]{1,0:T(8,128)S(1)}, f32[128,256]{1,0:T(8,128)S(1)}, u32[]{:S(2)}, u32[]{:S(2)}) collective-permute-start(f32[128,256]{1,0:T(8,128)S(1)} %get-tuple-element.17), channel_id=1, source_target_pairs={{0,128},{8,136},{16,144},{24,152},{32,160},{40,168},{48,176},{56,1... | collective-permute-start | bytes 393224 | tf_op jit(solution)/shard_map/ppermute | solution.py:37
  44.8 2.9 %collective-permute-start.14 = (f32[832,128]{1,0:T(8,128)S(1)}, f32[832,128]{1,0:T(8,128)S(1)}, u32[]{:S(2)}, u32[]{:S(2)}) collective-permute-start(f32[832,128]{1,0:T(8,128)S(1)} %get-tuple-element.20), channel_id=1, source_target_pairs={{0,32},{8,40},{16,48},{24,56},{32,0},{40,8},{48,16},{56,24},{64,96... | collective-permute-start | bytes 1277960 | tf_op jit(solution)/shard_map/ppermute | solution.py:254
  48.1 2.3 %collective-permute-start.16 = (f32[832,128]{1,0:T(8,128)S(1)}, f32[832,128]{1,0:T(8,128)S(1)}, u32[]{:S(2)}, u32[]{:S(2)}) collective-permute-start(f32[832,128]{1,0:T(8,128)S(1)} %get-tuple-element.22), channel_id=1, source_target_pairs={{0,48},{8,56},{16,0},{24,8},{32,16},{40,24},{48,32},{56,40},{64,11... | collective-permute-start | bytes 1277960 | tf_op jit(solution)/shard_map/ppermute | solution.py:254
  50.7 2.4 %collective-permute-start.13 = (f32[128,256]{1,0:T(8,128)S(1)}, f32[128,256]{1,0:T(8,128)S(1)}, u32[]{:S(2)}, u32[]{:S(2)}) collective-permute-start(f32[128,256]{1,0:T(8,128)S(1)} %get-tuple-element.17), channel_id=1, source_target_pairs={{0,192},{8,200},{16,208},{24,216},{32,224},{40,232},{48,240},{56,2... | collective-permute-start | bytes 393224 | tf_op jit(solution)/shard_map/ppermute | solution.py:37
  53.0 2.6 %collective-permute-done.12 = f32[128,256]{1,0:T(8,128)S(1)} collective-permute-done((f32[128,256]{1,0:T(8,128)S(1)}, f32[128,256]{1,0:T(8,128)S(1)}, u32[]{:S(2)}, u32[]{:S(2)}) %collective-permute-start.12) | collective-permute-done | bytes 131104 | tf_op jit(solution)/shard_map/ppermute | solution.py:37
  57.1 2.7 %collective-permute-start.23 = (f32[128,256]{1,0:T(8,128)S(1)}, f32[128,256]{1,0:T(8,128)S(1)}, u32[]{:S(2)}, u32[]{:S(2)}) collective-permute-start(f32[128,256]{1,0:T(8,128)S(1)} %add_add_fusion.1), channel_id=1, source_target_pairs={{0,48},{8,56},{16,0},{24,8},{32,16},{40,24},{48,32},{56,40},{64,11... | collective-permute-start | bytes 393224 | tf_op jit(solution)/shard_map/ppermute | solution.py:37
  59.8 8.3 %collective-permute-done.15 = f32[832,128]{1,0:T(8,128)S(1)} collective-permute-done((f32[832,128]{1,0:T(8,128)S(1)}, f32[832,128]{1,0:T(8,128)S(1)}, u32[]{:S(2)}, u32[]{:S(2)}) %collective-permute-start.15) | collective-permute-done | bytes 426016 | tf_op jit(solution)/shard_map/ppermute | solution.py:254
  69.8 1.5 collective-permute-start.19
  71.2 1.5 collective-permute-done.22
  73.8 2.6 %collective-permute-done.18 = f32[208,128]{1,0:T(8,128)S(1)} collective-permute-done((f32[208,128]{1,0:T(8,128)S(1)}, f32[208,128]{1,0:T(8,128)S(1)}, u32[]{:S(2)}, u32[]{:S(2)}) %collective-permute-start.18) | collective-permute-done | bytes 106528 | tf_op jit(solution)/shard_map/ppermute | solution.py:263
  77.6 49.4 %inverse_factor.1 = f32[256,256]{1,0:T(8,128)S(1)} custom-call(s32[3]{0:T(128)S(1)} %pad_add_fusion.place_ref.core_ref, f32[128,256]{1,0:T(8,128)S(1)} %add_add_fusion.own_ref, f32[128,256]{1,0:T(8,128)S(1)} %collective-permute-done.24.other_ref), custom_call_target="tpu_custom_call" | custom-call | flops 5000000000 | bytes 600000 | tf_op jit(solution)/shard_map/inverse_factor/pallas_call | solution.py:103
  127.6 19.6 %all_to_all.5 = bf16[16,208,128]{2,1,0:T(8,128)(2,1)S(1)} all-to-all(bf16[16,208,128]{2,1,0:T(8,128)(2,1)S(1)} %broadcast_in_dim.6), channel_id=1, replica_groups={{0,64,128,192,16,80,144,208,32,96,160,224,48,112,176,240},{8,72,136,200..., dimensions={0} | all-to-all | bytes 1703936 | tf_op jit(solution)/shard_map/all_to_all | solution.py:271
  149.1 1.7 %collective-permute-start.25 = (f32[1,128]{1,0:T(1,128)S(1)}, f32[1,128]{1,0:T(1,128)S(1)}, u32[]{:S(2)}, u32[]{:S(2)}) collective-permute-start(f32[1,128]{1,0:T(1,128)S(1)} %bitcast.17), channel_id=1, source_target_pairs={{0,1},{1,0},{2,3},{3,2},{4,5},{5,4},{6,7},{7,6},{8,9},{9,8},{10,11... | collective-permute-start | bytes 1544 | tf_op jit(solution)/shard_map/ppermute | solution.py:279
  151.8 2.1 %collective-permute-start.26 = (f32[1,128]{1,0:T(1,128)S(1)}, f32[1,128]{1,0:T(1,128)S(1)}, u32[]{:S(2)}, u32[]{:S(2)}) collective-permute-start(f32[1,128]{1,0:T(1,128)S(1)} %bitcast_add_fusion), channel_id=1, source_target_pairs={{0,2},{1,3},{2,0},{3,1},{4,6},{5,7},{6,4},{7,5},{8,10},{9,11},{10,... | collective-permute-start | bytes 1544 | tf_op jit(solution)/shard_map/ppermute | solution.py:279
  155.1 5.2 %collective-permute-start.27 = (f32[1,128]{1,0:T(1,128)S(1)}, f32[1,128]{1,0:T(1,128)S(1)}, u32[]{:S(2)}, u32[]{:S(2)}) collective-permute-start(f32[1,128]{1,0:T(1,128)S(1)} %add.253), channel_id=1, source_target_pairs={{0,7},{1,6},{2,5},{3,4},{4,3},{5,2},{6,1},{7,0},{8,15},{9,14},{10,... | collective-permute-start | bytes 1544 | tf_op jit(solution)/shard_map/ppermute | solution.py:279
  160.3 2.3 %fusion.2 = bf16[256,3328]{1,0:T(8,128)(2,1)} fusion(bf16[256,256]{1,0:T(8,128)(2,1)S(1)} %convolution_convert_fusion, bf16[256,3328]{1,0:T(8,128)(2,1)S(1)} %copy-done.4, bf16[256,3328]{1,0:T(8,128)(2,1)S(1)} %copy-done.2, bf16[3328,128]{1,0:T(8,128)(2,1)S(1)} %collective-permute-done.28, bf16[3328,128]{1,0:T(8,128)(2,1)S(1)} %bitcast.15, pred[]{:T(512)S(6)} %eq.25), kind=kOutput, calls=%fused_computation.4 | convolution fusion | flops 448987136 | bytes 6946817 | tf_op jit(solution)/shard_map/dot_general | solution.py:275
  162.6 2.6 %collective-permute-start.29 = (f32[1,128]{1,0:T(1,128)S(1)}, f32[1,128]{1,0:T(1,128)S(1)}, u32[]{:S(2)}, u32[]{:S(2)}) collective-permute-start(f32[1,128]{1,0:T(1,128)S(1)} %add.255), channel_id=1, source_target_pairs={{0,8},{8,0},{16,24},{24,16},{32,40},{40,32},{48,56},{56,48},{64,72... | collective-permute-start | bytes 1544 | tf_op jit(solution)/shard_map/ppermute | solution.py:283
  167.4 1.8 %fusion.3 = bf16[256,3328]{1,0:T(8,128)(2,1)} fusion(bf16[256,256]{1,0:T(8,128)(2,1)S(1)} %convolution_convert_fusion, bf16[3328,256]{1,0:T(8,128)(2,1)S(1)} %multiply_convert_fusion, bf16[256,3328]{1,0:T(8,128)(2,1)S(1)} %copy-done.6), kind=kOutput, calls=%fused_computation.5 | convolution fusion | flops 439615488 | bytes 5242880 | tf_op jit(solution)/shard_map/dot_general | solution.py:285
  (67 shorter events, 18.1 us)
Async XLA Ops:
  6.3 30.9 %collective-permute-start = (bf16[256,3328]{1,0:T(8,128)(2,1)S(1)}, bf16[256,3328]{1,0:T(8,128)(2,1)}, u32[]{:S(2)}, u32[]{:S(2)}) collective-permute-start(bf16[256,3328]{1,0:T(8,128)(2,1)S(1)} %get-tuple-element.15.s_ref), channel_id=1, source_target_pairs={{0,8},{8,0},{16,24},{24,16},{32,40},{40,32},{48,56},{56,48},{64,72... | collective-permute-start | bytes 5111816 | tf_op jit(solution)/shard_map/ppermute | solution.py:244
  7.1 5.4 %collective-permute-start.1 = (f32[128,256]{1,0:T(8,128)S(1)}, f32[128,256]{1,0:T(8,128)S(1)}, u32[]{:S(2)}, u32[]{:S(2)}) collective-permute-start(f32[128,256]{1,0:T(8,128)S(1)} %constant_dynamic-slice_fusion), channel_id=1, source_target_pairs={{0,1},{1,0},{2,3},{3,2},{4,5},{5,4},{6,7},{7,6},{8,9},{9,8},{10,11... | collective-permute-start | bytes 393224 | tf_op jit(solution)/shard_map/ppermute | solution.py:218
  12.5 4.6 %collective-permute-start.2 = (f32[64,256]{1,0:T(8,128)S(1)}, f32[64,256]{1,0:T(8,128)S(1)}, u32[]{:S(2)}, u32[]{:S(2)}) collective-permute-start(f32[64,256]{1,0:T(8,128)S(1)} %dynamic-slice_add_fusion), channel_id=1, source_target_pairs={{0,2},{1,3},{2,0},{3,1},{4,6},{5,7},{6,4},{7,5},{8,10},{9,11},{10,... | collective-permute-start | bytes 196616 | tf_op jit(solution)/shard_map/ppermute | solution.py:219
  17.1 6.9 %collective-permute-start.3 = (f32[64,256]{1,0:T(8,128)S(1)}, f32[64,256]{1,0:T(8,128)S(1)}, u32[]{:S(2)}, u32[]{:S(2)}) collective-permute-start(f32[64,256]{1,0:T(8,128)S(1)} %add_add_fusion.6), channel_id=1, source_target_pairs={{0,7},{1,6},{2,5},{3,4},{4,3},{5,2},{6,1},{7,0},{8,15},{9,14},{10,... | collective-permute-start | bytes 196616 | tf_op jit(solution)/shard_map/ppermute | solution.py:225
  24.0 4.2 %collective-permute-start.4 = (f32[64,256]{1,0:T(8,128)S(1)}, f32[64,256]{1,0:T(8,128)S(1)}, u32[]{:S(2)}, u32[]{:S(2)}) collective-permute-start(f32[64,256]{1,0:T(8,128)S(1)} %add.218.refs_0_), channel_id=1, source_target_pairs={{0,2},{1,3},{2,0},{3,1},{4,6},{5,7},{6,4},{7,5},{8,10},{9,11},{10,... | collective-permute-start | bytes 196616 | tf_op jit(solution)/shard_map/ppermute | solution.py:219
  25.5 8.4 %collective-permute-start.5 = (f32[64,256]{1,0:T(8,128)S(1)}, f32[64,256]{1,0:T(8,128)S(1)}, u32[]{:S(2)}, u32[]{:S(2)}) collective-permute-start(f32[64,256]{1,0:T(8,128)S(1)} %add.218.refs_0_), channel_id=1, source_target_pairs={{0,1},{1,0},{2,3},{3,2},{4,5},{5,4},{6,7},{7,6},{8,9},{9,8},{10,11... | collective-permute-start | bytes 196616 | tf_op jit(solution)/shard_map/ppermute | solution.py:218
  28.2 6.2 %collective-permute-start.6 = (f32[64,256]{1,0:T(8,128)S(1)}, f32[64,256]{1,0:T(8,128)S(1)}, u32[]{:S(2)}, u32[]{:S(2)}) collective-permute-start(f32[64,256]{1,0:T(8,128)S(1)} %collective-permute-done.4.refs_1_), channel_id=1, source_target_pairs={{0,1},{1,0},{2,3},{3,2},{4,5},{5,4},{6,7},{7,6},{8,9},{9,8},{10,11... | collective-permute-start | bytes 196616 | tf_op jit(solution)/shard_map/ppermute | solution.py:218
  29.8 6.6 %collective-permute-start.7 = (f32[64,256]{1,0:T(8,128)S(1)}, f32[64,256]{1,0:T(8,128)S(1)}, u32[]{:S(2)}, u32[]{:S(2)}) collective-permute-start(f32[64,256]{1,0:T(8,128)S(1)} %add.218.refs_0_), channel_id=1, source_target_pairs={{0,8},{8,0},{16,24},{24,16},{32,40},{40,32},{48,56},{56,48},{64,72... | collective-permute-start | bytes 196616 | tf_op jit(solution)/shard_map/ppermute | solution.py:246
  34.0 2.4 %collective-permute-start.8 = (f32[64,256]{1,0:T(8,128)S(1)}, f32[64,256]{1,0:T(8,128)S(1)}, u32[]{:S(2)}, u32[]{:S(2)}) collective-permute-start(f32[64,256]{1,0:T(8,128)S(1)} %collective-permute-done.4.refs_1_), channel_id=1, source_target_pairs={{0,8},{8,0},{16,24},{24,16},{32,40},{40,32},{48,56},{56,48},{64,72... | collective-permute-start | bytes 196616 | tf_op jit(solution)/shard_map/ppermute | solution.py:246
  34.0 2.4 %collective-permute-start.9 = (f32[64,256]{1,0:T(8,128)S(1)}, f32[64,256]{1,0:T(8,128)S(1)}, u32[]{:S(2)}, u32[]{:S(2)}) collective-permute-start(f32[64,256]{1,0:T(8,128)S(1)} %collective-permute-done.5.refs_2_), channel_id=1, source_target_pairs={{0,8},{8,0},{16,24},{24,16},{32,40},{40,32},{48,56},{56,48},{64,72... | collective-permute-start | bytes 196616 | tf_op jit(solution)/shard_map/ppermute | solution.py:246
  34.5 2.7 %collective-permute-start.10 = (f32[64,256]{1,0:T(8,128)S(1)}, f32[64,256]{1,0:T(8,128)S(1)}, u32[]{:S(2)}, u32[]{:S(2)}) collective-permute-start(f32[64,256]{1,0:T(8,128)S(1)} %collective-permute-done.6.refs_3_), channel_id=1, source_target_pairs={{0,8},{8,0},{16,24},{24,16},{32,40},{40,32},{48,56},{56,48},{64,72... | collective-permute-start | bytes 196616 | tf_op jit(solution)/shard_map/ppermute | solution.py:246
  41.9 8.7 %collective-permute-start.11 = (f32[128,256]{1,0:T(8,128)S(1)}, f32[128,256]{1,0:T(8,128)S(1)}, u32[]{:S(2)}, u32[]{:S(2)}) collective-permute-start(f32[128,256]{1,0:T(8,128)S(1)} %get-tuple-element.17), channel_id=1, source_target_pairs={{0,128},{8,136},{16,144},{24,152},{32,160},{40,168},{48,176},{56,1... | collective-permute-start | bytes 393224 | tf_op jit(solution)/shard_map/ppermute | solution.py:37
  44.8 12.3 %collective-permute-start.14 = (f32[832,128]{1,0:T(8,128)S(1)}, f32[832,128]{1,0:T(8,128)S(1)}, u32[]{:S(2)}, u32[]{:S(2)}) collective-permute-start(f32[832,128]{1,0:T(8,128)S(1)} %get-tuple-element.20), channel_id=1, source_target_pairs={{0,32},{8,40},{16,48},{24,56},{32,0},{40,8},{48,16},{56,24},{64,96... | collective-permute-start | bytes 1277960 | tf_op jit(solution)/shard_map/ppermute | solution.py:254
  47.7 20.4 %collective-permute-start.15 = (f32[832,128]{1,0:T(8,128)S(1)}, f32[832,128]{1,0:T(8,128)S(1)}, u32[]{:S(2)}, u32[]{:S(2)}) collective-permute-start(f32[832,128]{1,0:T(8,128)S(1)} %get-tuple-element.21), channel_id=1, source_target_pairs={{0,16},{8,24},{16,32},{24,40},{32,48},{40,56},{48,0},{56,8},{64,80... | collective-permute-start | bytes 1277960 | tf_op jit(solution)/shard_map/ppermute | solution.py:254
  48.1 20.0 %collective-permute-start.16 = (f32[832,128]{1,0:T(8,128)S(1)}, f32[832,128]{1,0:T(8,128)S(1)}, u32[]{:S(2)}, u32[]{:S(2)}) collective-permute-start(f32[832,128]{1,0:T(8,128)S(1)} %get-tuple-element.22), channel_id=1, source_target_pairs={{0,48},{8,56},{16,0},{24,8},{32,16},{40,24},{48,32},{56,40},{64,11... | collective-permute-start | bytes 1277960 | tf_op jit(solution)/shard_map/ppermute | solution.py:254
  50.4 5.3 %collective-permute-start.12 = (f32[128,256]{1,0:T(8,128)S(1)}, f32[128,256]{1,0:T(8,128)S(1)}, u32[]{:S(2)}, u32[]{:S(2)}) collective-permute-start(f32[128,256]{1,0:T(8,128)S(1)} %get-tuple-element.17), channel_id=1, source_target_pairs={{0,64},{8,72},{16,80},{24,88},{32,96},{40,104},{48,112},{56,120},{... | collective-permute-start | bytes 393224 | tf_op jit(solution)/shard_map/ppermute | solution.py:37
  50.7 5.0 %collective-permute-start.13 = (f32[128,256]{1,0:T(8,128)S(1)}, f32[128,256]{1,0:T(8,128)S(1)}, u32[]{:S(2)}, u32[]{:S(2)}) collective-permute-start(f32[128,256]{1,0:T(8,128)S(1)} %get-tuple-element.17), channel_id=1, source_target_pairs={{0,192},{8,200},{16,208},{24,216},{32,224},{40,232},{48,240},{56,2... | collective-permute-start | bytes 393224 | tf_op jit(solution)/shard_map/ppermute | solution.py:37
  55.7 14.0 %collective-permute-start.21 = (f32[128,256]{1,0:T(8,128)S(1)}, f32[128,256]{1,0:T(8,128)S(1)}, u32[]{:S(2)}, u32[]{:S(2)}) collective-permute-start(f32[128,256]{1,0:T(8,128)S(1)} %add_add_fusion.1), channel_id=1, source_target_pairs={{0,32},{8,40},{16,48},{24,56},{32,0},{40,8},{48,16},{56,24},{64,96... | collective-permute-start | bytes 393224 | tf_op jit(solution)/shard_map/ppermute | solution.py:37
  55.8 16.9 %collective-permute-start.22 = (f32[128,256]{1,0:T(8,128)S(1)}, f32[128,256]{1,0:T(8,128)S(1)}, u32[]{:S(2)}, u32[]{:S(2)}) collective-permute-start(f32[128,256]{1,0:T(8,128)S(1)} %add_add_fusion.1), channel_id=1, source_target_pairs={{0,16},{8,24},{16,32},{24,40},{32,48},{40,56},{48,0},{56,8},{64,80... | collective-permute-start | bytes 393224 | tf_op jit(solution)/shard_map/ppermute | solution.py:37
  57.1 15.7 %collective-permute-start.23 = (f32[128,256]{1,0:T(8,128)S(1)}, f32[128,256]{1,0:T(8,128)S(1)}, u32[]{:S(2)}, u32[]{:S(2)}) collective-permute-start(f32[128,256]{1,0:T(8,128)S(1)} %add_add_fusion.1), channel_id=1, source_target_pairs={{0,48},{8,56},{16,0},{24,8},{32,16},{40,24},{48,32},{56,40},{64,11... | collective-permute-start | bytes 393224 | tf_op jit(solution)/shard_map/ppermute | solution.py:37
  68.2 5.6 %collective-permute-start.17 = (f32[208,128]{1,0:T(8,128)S(1)}, f32[208,128]{1,0:T(8,128)S(1)}, u32[]{:S(2)}, u32[]{:S(2)}) collective-permute-start(f32[208,128]{1,0:T(8,128)S(1)} %get-tuple-element.27), channel_id=1, source_target_pairs={{0,128},{8,136},{16,144},{24,152},{32,160},{40,168},{48,176},{56,1... | collective-permute-start | bytes 319496 | tf_op jit(solution)/shard_map/ppermute | solution.py:262
  68.5 7.9 %collective-permute-start.18 = (f32[208,128]{1,0:T(8,128)S(1)}, f32[208,128]{1,0:T(8,128)S(1)}, u32[]{:S(2)}, u32[]{:S(2)}) collective-permute-start(f32[208,128]{1,0:T(8,128)S(1)} %get-tuple-element.29), channel_id=1, source_target_pairs={{0,64},{8,72},{16,80},{24,88},{32,96},{40,104},{48,112},{56,120},{... | collective-permute-start | bytes 319496 | tf_op jit(solution)/shard_map/ppermute | solution.py:263
  69.8 6.7 %collective-permute-start.19 = (f32[208,128]{1,0:T(8,128)S(1)}, f32[208,128]{1,0:T(8,128)S(1)}, u32[]{:S(2)}, u32[]{:S(2)}) collective-permute-start(f32[208,128]{1,0:T(8,128)S(1)} %get-tuple-element.28), channel_id=1, source_target_pairs={{0,192},{8,200},{16,208},{24,216},{32,224},{40,232},{48,240},{56,2... | collective-permute-start | bytes 319496 | tf_op jit(solution)/shard_map/ppermute | solution.py:263
  72.8 4.8 %collective-permute-start.24 = (f32[128,256]{1,0:T(8,128)S(1)}, f32[128,256]{1,0:T(8,128)S(1)}, u32[]{:S(2)}, u32[]{:S(2)}) collective-permute-start(f32[128,256]{1,0:T(8,128)S(1)} %add_add_fusion.own_ref), channel_id=1, source_target_pairs={{0,8},{8,0},{16,24},{24,16},{32,40},{40,32},{48,56},{56,48},{64,72... | collective-permute-start | bytes 393224 | tf_op jit(solution)/shard_map/ppermute | solution.py:264
  76.5 50.5 %collective-permute-start.20 = (f32[208,128]{1,0:T(8,128)S(1)}, f32[208,128]{1,0:T(8,128)S(1)}, u32[]{:S(2)}, u32[]{:S(2)}) collective-permute-start(f32[208,128]{1,0:T(8,128)S(1)} %add_add_fusion.2), channel_id=1, source_target_pairs={{0,8},{8,0},{16,24},{24,16},{32,40},{40,32},{48,56},{56,48},{64,72... | collective-permute-start | bytes 319496 | tf_op jit(solution)/shard_map/ppermute | solution.py:265
  127.5 32.8 %copy-start.4 = (bf16[256,3328]{1,0:T(8,128)(2,1)S(1)}, bf16[256,3328]{1,0:T(8,128)(2,1)}, u32[]{:S(2)}) copy-start(bf16[256,3328]{1,0:T(8,128)(2,1)} %g_ref.1) | copy-start | bytes 5111812
  127.6 32.7 %copy-start.2 = (bf16[256,3328]{1,0:T(8,128)(2,1)S(1)}, bf16[256,3328]{1,0:T(8,128)(2,1)}, u32[]{:S(2)}) copy-start(bf16[256,3328]{1,0:T(8,128)(2,1)} %m_ref.1) | copy-start | bytes 5111812
  147.2 13.0 %collective-permute-start.28 = (bf16[3328,128]{1,0:T(8,128)(2,1)S(1)}, bf16[3328,128]{1,0:T(8,128)(2,1)S(1)}, u32[]{:S(2)}, u32[]{:S(2)}) collective-permute-start(bf16[3328,128]{1,0:T(8,128)(2,1)S(1)} %bitcast.14), channel_id=1, source_target_pairs={{0,8},{8,0},{16,24},{24,16},{32,40},{40,32},{48,56},{56,48},{64,72... | collective-permute-start | bytes 2555912 | tf_op jit(solution)/shard_map/ppermute | solution.py:274
  149.1 2.7 %collective-permute-start.25 = (f32[1,128]{1,0:T(1,128)S(1)}, f32[1,128]{1,0:T(1,128)S(1)}, u32[]{:S(2)}, u32[]{:S(2)}) collective-permute-start(f32[1,128]{1,0:T(1,128)S(1)} %bitcast.17), channel_id=1, source_target_pairs={{0,1},{1,0},{2,3},{3,2},{4,5},{5,4},{6,7},{7,6},{8,9},{9,8},{10,11... | collective-permute-start | bytes 1544 | tf_op jit(solution)/shard_map/ppermute | solution.py:279
  151.8 3.3 %collective-permute-start.26 = (f32[1,128]{1,0:T(1,128)S(1)}, f32[1,128]{1,0:T(1,128)S(1)}, u32[]{:S(2)}, u32[]{:S(2)}) collective-permute-start(f32[1,128]{1,0:T(1,128)S(1)} %bitcast_add_fusion), channel_id=1, source_target_pairs={{0,2},{1,3},{2,0},{3,1},{4,6},{5,7},{6,4},{7,5},{8,10},{9,11},{10,... | collective-permute-start | bytes 1544 | tf_op jit(solution)/shard_map/ppermute | solution.py:279
  155.1 7.5 %collective-permute-start.27 = (f32[1,128]{1,0:T(1,128)S(1)}, f32[1,128]{1,0:T(1,128)S(1)}, u32[]{:S(2)}, u32[]{:S(2)}) collective-permute-start(f32[1,128]{1,0:T(1,128)S(1)} %add.253), channel_id=1, source_target_pairs={{0,7},{1,6},{2,5},{3,4},{4,3},{5,2},{6,1},{7,0},{8,15},{9,14},{10,... | collective-permute-start | bytes 1544 | tf_op jit(solution)/shard_map/ppermute | solution.py:279
  162.6 3.4 %collective-permute-start.29 = (f32[1,128]{1,0:T(1,128)S(1)}, f32[1,128]{1,0:T(1,128)S(1)}, u32[]{:S(2)}, u32[]{:S(2)}) collective-permute-start(f32[1,128]{1,0:T(1,128)S(1)} %add.255), channel_id=1, source_target_pairs={{0,8},{8,0},{16,24},{24,16},{32,40},{40,32},{48,56},{56,48},{64,72... | collective-permute-start | bytes 1544 | tf_op jit(solution)/shard_map/ppermute | solution.py:283
  (5 other events, 7.7 us)

commit v4 on v3

--- a/solution.py
+++ b/solution.py
@@ -211,6 +211,48 @@
     )(now, summed_b, summed_o, *pieces)
 
 
+FACTOR = 0.2 * math.sqrt(D * FF / RANK)
+
+
+def finish_kernel(place_ref, own_ref, other_ref, colsq_ref, ortho_ref, weight_ref, basis_ref, out_ref):
+    first = place_ref[0] == 0
+    own, other = own_ref[...].astype(f32), other_ref[...].astype(f32)
+    right = jnp.concatenate([jnp.where(first, own, other), jnp.where(first, other, own)], axis=1)
+    basis = (right * lax.rsqrt(colsq_ref[...] + 1e-06)).astype(bf16)
+    basis_ref[...] = basis
+    update = lax.dot_general(
+        ortho_ref[...], basis, (((1,), (1,)), ((), ())), preferred_element_type=f32
+    )
+    out_ref[...] = (weight_ref[...].astype(f32) - FACTOR * update).astype(bf16)
+
+
+def finish(now, own, other, colsq, ortho, weight):
+    columns = pl.BlockSpec((256, WIDE), lambda i, p: (0, i))
+    half = pl.BlockSpec((WIDE, HALF), lambda i, p: (i, 0))
+    return pl.pallas_call(
+        finish_kernel,
+        grid_spec=pltpu.PrefetchScalarGridSpec(
+            num_scalar_prefetch=1,
+            grid=(2,),
+            in_specs=[
+                half,
+                half,
+                pl.BlockSpec((1, RANK), lambda i, p: (0, 0)),
+                pl.BlockSpec((256, RANK), lambda i, p: (0, 0)),
+                columns,
+            ],
+            out_specs=[pl.BlockSpec((WIDE, RANK), lambda i, p: (i, 0)), columns],
+        ),
+        out_shape=[
+            jax.ShapeDtypeStruct((3328, RANK), bf16),
+            jax.ShapeDtypeStruct((256, 3328), bf16),
+        ],
+        compiler_params=pltpu.CompilerParams(vmem_limit_bytes=24 * 1024 * 1024),
+        cost_estimate=pl.CostEstimate(flops=440_000_000, bytes_accessed=7_000_000, transcendentals=0),
+        name="finish",
+    )(now, own, other, colsq, ortho, weight)
+
+
 def sum_over_z(part):
     z = lax.axis_index(T)
     label = jnp.where(z < 4, z, 7 - z)
@@ -271,7 +313,8 @@
     right = lax.all_to_all(
         jnp.broadcast_to(right, (16, 208, HALF)), F, 0, 0, axis_index_groups=PLANE
     ).reshape(3328, HALF)
-    right_b = join(right, lax.ppermute(right, F, CORE))
+    right_o = lax.ppermute(right, F, CORE)
+    right_b = join(right, right_o)
     back = lax.dot_general(ortho, right_b, over_rank, preferred_element_type=f32)
     momentum_new = (summed - 0.05 * back).astype(bf16)
     colsq = jnp.sum(jnp.square(right.astype(f32)), axis=0, keepdims=True)
@@ -281,10 +324,7 @@
             got, momentum_new = lax.optimization_barrier((got, momentum_new))
         colsq = colsq + got
     colsq = join(colsq, lax.ppermute(colsq, F, CORE))
-    basis_new = (right_b.astype(f32) * lax.rsqrt(colsq + 1e-06)).astype(bf16)
-    update = lax.dot_general(ortho, basis_new, over_rank, preferred_element_type=f32)
-    factor = 0.2 * math.sqrt(D * FF / RANK)
-    weight_new = (weight.astype(f32) - factor * update).astype(bf16)
+    basis_new, weight_new = finish(now, right, right_o, colsq, ortho, weight)
     return (momentum_new, weight_new, basis_new)
 
 

time: 170 us -> 169 us (level)
  Pallas kernels: 55.4 us -> 58.9 us
  waiting for transfers between devices: 28.8 us -> 30.9 us
  starting transfers between devices: 52.9 us -> 50.9 us
  matrix products: 4.94 us -> 3.15 us
    ppermute x6, waiting for transfers between devices: 4.2 us -> 8.49 us  [ring_sum(): one, two, three = [lax.ppermute(v, F, s) for s in shifts]]
    pallas_call x0 -> x1, Pallas kernels: none -> 2.8 us  [finish(): pl.pallas_call(finish_kernel, grid_spec=pltpu.PrefetchScalarGridSpec(num_...]
    ppermute x6, starting transfers between devices: 8.91 us -> 6.72 us  [ring_sum(): one, two, three = [lax.ppermute(v, F, s) for s in shifts]]
    dot_general x1 -> x0, matrix products: 1.83 us -> none  [local(): lax.dot_general(ortho, basis_new, over_rank, preferred_element_type=f32)]
    ppermute x3, waiting for transfers between devices: 8.95 us -> 7.14 us  [local(): us = [us[0]] + [lax.ppermute(us[k], F, YS[k - 1]) for k in (1, 2, 3)]]
    ppermute x2, starting transfers between devices: 2.68 us -> 0.86 us  [local(): u = u + (lax.ppermute(vs[1], F, XS[0]) + lax.ppermute(vs[3], F, XS[2]))]
    unnamed x14 -> x12, local copies, waits for them, and re-layouts: 4.63 us -> 4.37 us
  transfers between devices with their start and end apart: 30 -> 30, of which waited for: 13 -> 14; matrix products, arithmetic and copies ran while one was open for 2% -> 2% of each run, Pallas kernels for 29% -> 30%
where the time goes in v4:
time: 169 us; the launch traced here: 168 us
  Pallas kernels  58.9 us (35%)
  starting transfers between devices  50.9 us (30%)
  waiting for transfers between devices  30.9 us (18%)
  blocking collectives  18.4 us (11%)
  local copies, waits for them, and re-layouts  4.5 us (3%)
  matrix products  3.15 us (2%)
    pallas_call x1, Pallas kernels, inverse_factor(): pl.pallas_call(inverse_kernel, out_shape=jax.ShapeDtypeStruct((RANK, RANK...  50.1 us
    all_to_all x1, blocking collectives, local(): lax.all_to_all(jnp.broadcast_to(right, (16, 208, HALF)), F, 0, 0, axis_in...  18.4 us
    ppermute x3, starting transfers between devices, local(): got = lax.ppermute(colsq, T, s)  8.96 us
    ppermute x6, waiting for transfers between devices, ring_sum(): one, two, three = [lax.ppermute(v, F, s) for s in shifts]  8.49 us
    ppermute x3, waiting for transfers between devices, local(): us = [us[0]] + [lax.ppermute(us[k], F, YS[k - 1]) for k in (1, 2, 3)]  7.14 us
    ppermute x6, starting transfers between devices, ring_sum(): one, two, three = [lax.ppermute(v, F, s) for s in shifts]  6.72 us
    ppermute x4, starting transfers between devices, local(): others = [lax.ppermute(p, F, CORE) for p in pieces]  6.5 us
    ppermute x3, starting transfers between devices, local(): us = [us[0]] + [lax.ppermute(us[k], F, YS[k - 1]) for k in (1, 2, 3)]  5.59 us
  transfers between devices with their start and end apart: 30, of which 14 were waited for; matrix products, arithmetic and copies ran while one was open for 2% of the time, Pallas kernels for 30%

profile of v4, /device:TPU:33, one launch (start us, length us, event | category | flops | bytes accessed | tf_op | source)
XLA Modules:
  0.0 168.4 jit_solution(16252275373337759942)
XLA Ops:
  2.1 1.5 copy-done.1
  3.5 1.5 copy-done.3
  7.1 1.7 collective-permute-start.1
  8.7 3.7 %collective-permute-done.1 = f32[128,256]{1,0:T(8,128)S(1)} collective-permute-done((f32[128,256]{1,0:T(8,128)S(1)}, f32[128,256]{1,0:T(8,128)S(1)}, u32[]{:S(2)}, u32[]{:S(2)}) %collective-permute-start.1) | collective-permute-done | bytes 131104 | tf_op jit(solution)/shard_map/ppermute | solution.py:260
  12.5 2.9 %collective-permute-start.2 = (f32[64,256]{1,0:T(8,128)S(1)}, f32[64,256]{1,0:T(8,128)S(1)}, u32[]{:S(2)}, u32[]{:S(2)}) collective-permute-start(f32[64,256]{1,0:T(8,128)S(1)} %dynamic-slice_add_fusion), channel_id=1, source_target_pairs={{0,2},{1,3},{2,0},{3,1},{4,6},{5,7},{6,4},{7,5},{8,10},{9,11},{10,... | collective-permute-start | bytes 196616 | tf_op jit(solution)/shard_map/ppermute | solution.py:261
  15.3 1.8 %collective-permute-done.2 = f32[64,256]{1,0:T(8,128)S(1)} collective-permute-done((f32[64,256]{1,0:T(8,128)S(1)}, f32[64,256]{1,0:T(8,128)S(1)}, u32[]{:S(2)}, u32[]{:S(2)}) %collective-permute-start.2) | collective-permute-done | bytes 65568 | tf_op jit(solution)/shard_map/ppermute | solution.py:261
  17.1 5.0 %collective-permute-start.3 = (f32[64,256]{1,0:T(8,128)S(1)}, f32[64,256]{1,0:T(8,128)S(1)}, u32[]{:S(2)}, u32[]{:S(2)}) collective-permute-start(f32[64,256]{1,0:T(8,128)S(1)} %add_add_fusion.6), channel_id=1, source_target_pairs={{0,7},{1,6},{2,5},{3,4},{4,3},{5,2},{6,1},{7,0},{8,15},{9,14},{10,... | collective-permute-start | bytes 196616 | tf_op jit(solution)/shard_map/ppermute | solution.py:267
  22.1 1.9 %collective-permute-done.3 = f32[64,256]{1,0:T(8,128)S(1)} collective-permute-done((f32[64,256]{1,0:T(8,128)S(1)}, f32[64,256]{1,0:T(8,128)S(1)}, u32[]{:S(2)}, u32[]{:S(2)}) %collective-permute-start.3) | collective-permute-done | bytes 65568 | tf_op jit(solution)/shard_map/ppermute | solution.py:267
  24.0 1.5 collective-permute-start.4
  26.0 2.3 %collective-permute-done.4.refs_1_ = f32[64,256]{1,0:T(8,128)S(1)} collective-permute-done((f32[64,256]{1,0:T(8,128)S(1)}, f32[64,256]{1,0:T(8,128)S(1)}, u32[]{:S(2)}, u32[]{:S(2)}) %collective-permute-start.4) | collective-permute-done | bytes 65568 | tf_op jit(solution)/shard_map/ppermute | solution.py:261
  28.2 1.5 collective-permute-start.6
  29.8 4.2 %collective-permute-start.7 = (f32[64,256]{1,0:T(8,128)S(1)}, f32[64,256]{1,0:T(8,128)S(1)}, u32[]{:S(2)}, u32[]{:S(2)}) collective-permute-start(f32[64,256]{1,0:T(8,128)S(1)} %add.207.refs_0_), channel_id=1, source_target_pairs={{0,8},{8,0},{16,24},{24,16},{32,40},{40,32},{48,56},{56,48},{64,72... | collective-permute-start | bytes 196616 | tf_op jit(solution)/shard_map/ppermute | solution.py:288
  34.5 1.8 %collective-permute-start.10 = (f32[64,256]{1,0:T(8,128)S(1)}, f32[64,256]{1,0:T(8,128)S(1)}, u32[]{:S(2)}, u32[]{:S(2)}) collective-permute-start(f32[64,256]{1,0:T(8,128)S(1)} %collective-permute-done.6.refs_3_), channel_id=1, source_target_pairs={{0,8},{8,0},{16,24},{24,16},{32,40},{40,32},{48,56},{56,48},{64,72... | collective-permute-start | bytes 196616 | tf_op jit(solution)/shard_map/ppermute | solution.py:288
  37.2 4.7 %spread.1 = (f32[832,128]{1,0:T(8,128)S(1)}, f32[832,128]{1,0:T(8,128)S(1)}, f32[832,128]{1,0:T(8,128)S(1)}, f32[832,128]{1,0:T(8,128)S(1)}, f32[128,256]{1,0:T(8,128)S(1)}, /*index=5*/f32[256,256]{1,0:T(8,128)S(1)}) custom-call(s32[3]{0:T(128)S(1)} %pad_add_fusion.place_ref.core_ref, bf16[256,3328]{1,0:T(8,128)(2,1)S(1)} %get-tuple-element.17.s_ref, ...), custom_call_target="tpu_custom_call" | custom-call | flops 2000000000 | bytes 6000000 | tf_op jit(solution)/shard_map/spread/pallas_call | solution.py:193
  41.9 2.6 %collective-permute-start.13 = (f32[128,256]{1,0:T(8,128)S(1)}, f32[128,256]{1,0:T(8,128)S(1)}, u32[]{:S(2)}, u32[]{:S(2)}) collective-permute-start(f32[128,256]{1,0:T(8,128)S(1)} %get-tuple-element.19), channel_id=1, source_target_pairs={{0,192},{8,200},{16,208},{24,216},{32,224},{40,232},{48,240},{56,2... | collective-permute-start | bytes 393224 | tf_op jit(solution)/shard_map/ppermute | solution.py:37
  44.5 2.9 %collective-permute-start.14 = (f32[832,128]{1,0:T(8,128)S(1)}, f32[832,128]{1,0:T(8,128)S(1)}, u32[]{:S(2)}, u32[]{:S(2)}) collective-permute-start(f32[832,128]{1,0:T(8,128)S(1)} %get-tuple-element.22), channel_id=1, source_target_pairs={{0,32},{8,40},{16,48},{24,56},{32,0},{40,8},{48,16},{56,24},{64,96... | collective-permute-start | bytes 1277960 | tf_op jit(solution)/shard_map/ppermute | solution.py:296
  47.8 2.3 %collective-permute-start.16 = (f32[832,128]{1,0:T(8,128)S(1)}, f32[832,128]{1,0:T(8,128)S(1)}, u32[]{:S(2)}, u32[]{:S(2)}) collective-permute-start(f32[832,128]{1,0:T(8,128)S(1)} %get-tuple-element.24), channel_id=1, source_target_pairs={{0,48},{8,56},{16,0},{24,8},{32,16},{40,24},{48,32},{56,40},{64,11... | collective-permute-start | bytes 1277960 | tf_op jit(solution)/shard_map/ppermute | solution.py:296
  50.1 1.7 %collective-permute-start.11 = (f32[128,256]{1,0:T(8,128)S(1)}, f32[128,256]{1,0:T(8,128)S(1)}, u32[]{:S(2)}, u32[]{:S(2)}) collective-permute-start(f32[128,256]{1,0:T(8,128)S(1)} %get-tuple-element.19), channel_id=1, source_target_pairs={{0,128},{8,136},{16,144},{24,152},{32,160},{40,168},{48,176},{56,1... | collective-permute-start | bytes 393224 | tf_op jit(solution)/shard_map/ppermute | solution.py:37
  51.8 5.4 %collective-permute-done.12 = f32[128,256]{1,0:T(8,128)S(1)} collective-permute-done((f32[128,256]{1,0:T(8,128)S(1)}, f32[128,256]{1,0:T(8,128)S(1)}, u32[]{:S(2)}, u32[]{:S(2)}) %collective-permute-start.12) | collective-permute-done | bytes 131104 | tf_op jit(solution)/shard_map/ppermute | solution.py:37
  57.4 1.5 collective-permute-start.22
  59.7 7.1 %collective-permute-done.15 = f32[832,128]{1,0:T(8,128)S(1)} collective-permute-done((f32[832,128]{1,0:T(8,128)S(1)}, f32[832,128]{1,0:T(8,128)S(1)}, u32[]{:S(2)}, u32[]{:S(2)}) %collective-permute-start.15) | collective-permute-done | bytes 426016 | tf_op jit(solution)/shard_map/ppermute | solution.py:296
  71.6 1.6 collective-permute-start.24
  73.2 2.2 %collective-permute-done.18 = f32[208,128]{1,0:T(8,128)S(1)} collective-permute-done((f32[208,128]{1,0:T(8,128)S(1)}, f32[208,128]{1,0:T(8,128)S(1)}, u32[]{:S(2)}, u32[]{:S(2)}) %collective-permute-start.18) | collective-permute-done | bytes 106528 | tf_op jit(solution)/shard_map/ppermute | solution.py:305
  75.4 2.3 %collective-permute-start.20 = (f32[208,128]{1,0:T(8,128)S(1)}, f32[208,128]{1,0:T(8,128)S(1)}, u32[]{:S(2)}, u32[]{:S(2)}) collective-permute-start(f32[208,128]{1,0:T(8,128)S(1)} %add_add_fusion.2), channel_id=1, source_target_pairs={{0,8},{8,0},{16,24},{24,16},{32,40},{40,32},{48,56},{56,48},{64,72... | collective-permute-start | bytes 319496 | tf_op jit(solution)/shard_map/ppermute | solution.py:307
  77.7 50.1 %inverse_factor.1 = f32[256,256]{1,0:T(8,128)S(1)} custom-call(s32[3]{0:T(128)S(1)} %pad_add_fusion.place_ref.core_ref, f32[128,256]{1,0:T(8,128)S(1)} %add_add_fusion.own_ref, f32[128,256]{1,0:T(8,128)S(1)} %collective-permute-done.24.other_ref), custom_call_target="tpu_custom_call" | custom-call | flops 5000000000 | bytes 600000 | tf_op jit(solution)/shard_map/inverse_factor/pallas_call | solution.py:103
  128.5 18.4 %all_to_all.5 = bf16[16,208,128]{2,1,0:T(8,128)(2,1)S(1)} all-to-all(bf16[16,208,128]{2,1,0:T(8,128)(2,1)S(1)} %broadcast_in_dim.6), channel_id=1, replica_groups={{0,64,128,192,16,80,144,208,32,96,160,224,48,112,176,240},{8,72,136,200..., dimensions={0} | all-to-all | bytes 1703936 | tf_op jit(solution)/shard_map/all_to_all | solution.py:313
  148.7 1.7 %collective-permute-start.25 = (f32[1,128]{1,0:T(1,128)S(1)}, f32[1,128]{1,0:T(1,128)S(1)}, u32[]{:S(2)}, u32[]{:S(2)}) collective-permute-start(f32[1,128]{1,0:T(1,128)S(1)} %bitcast.13), channel_id=1, source_target_pairs={{0,1},{1,0},{2,3},{3,2},{4,5},{5,4},{6,7},{7,6},{8,9},{9,8},{10,11... | collective-permute-start | bytes 1544 | tf_op jit(solution)/shard_map/ppermute | solution.py:322
  151.4 2.1 %collective-permute-start.26 = (f32[1,128]{1,0:T(1,128)S(1)}, f32[1,128]{1,0:T(1,128)S(1)}, u32[]{:S(2)}, u32[]{:S(2)}) collective-permute-start(f32[1,128]{1,0:T(1,128)S(1)} %bitcast_add_fusion), channel_id=1, source_target_pairs={{0,2},{1,3},{2,0},{3,1},{4,6},{5,7},{6,4},{7,5},{8,10},{9,11},{10,... | collective-permute-start | bytes 1544 | tf_op jit(solution)/shard_map/ppermute | solution.py:322
  154.7 5.2 %collective-permute-start.27 = (f32[1,128]{1,0:T(1,128)S(1)}, f32[1,128]{1,0:T(1,128)S(1)}, u32[]{:S(2)}, u32[]{:S(2)}) collective-permute-start(f32[1,128]{1,0:T(1,128)S(1)} %add.242), channel_id=1, source_target_pairs={{0,7},{1,6},{2,5},{3,4},{4,3},{5,2},{6,1},{7,0},{8,15},{9,14},{10,... | collective-permute-start | bytes 1544 | tf_op jit(solution)/shard_map/ppermute | solution.py:322
  159.9 2.3 %fusion.1 = bf16[256,3328]{1,0:T(8,128)(2,1)} fusion(bf16[256,256]{1,0:T(8,128)(2,1)S(1)} %convolution_convert_fusion.ortho_ref, bf16[256,3328]{1,0:T(8,128)(2,1)S(1)} %copy-done.4, bf16[256,3328]{1,0:T(8,128)(2,1)S(1)} %copy-done.2, bf16[3328,128]{1,0:T(8,128)(2,1)S(1)} %collective-permute-done.28.other_ref, bf16[3328,128]{1,0:T(8,128)(2,1)S(1)} %bitcast.11, ...), kind=kOutput, calls=%fused_computation.2 | convolution fusion | flops 448987136 | bytes 6946817 | tf_op jit(solution)/shard_map/dot_general | solution.py:318
  162.2 2.6 %collective-permute-start.29 = (f32[1,128]{1,0:T(1,128)S(1)}, f32[1,128]{1,0:T(1,128)S(1)}, u32[]{:S(2)}, u32[]{:S(2)}) collective-permute-start(f32[1,128]{1,0:T(1,128)S(1)} %add.244), channel_id=1, source_target_pairs={{0,8},{8,0},{16,24},{24,16},{32,40},{40,32},{48,56},{56,48},{64,72... | collective-permute-start | bytes 1544 | tf_op jit(solution)/shard_map/ppermute | solution.py:326
  165.6 2.8 %finish.1 = (bf16[3328,256]{1,0:T(8,128)(2,1)}, bf16[256,3328]{1,0:T(8,128)(2,1)}) custom-call(s32[3]{0:T(128)S(1)} %pad_add_fusion.place_ref.core_ref, bf16[3328,128]{1,0:T(8,128)(2,1)S(1)} %bitcast.12, bf16[3328,128]{1,0:T(8,128)(2,1)S(1)} %collective-permute-done.28.other_ref, f32[1,256]{1,0:T(1,128)S(1)} %broadcast_select_fusion.colsq_ref, ...), custom_call_target="tpu_custom_call" | custom-call | flops 440000000 | bytes 7000000 | tf_op jit(solution)/shard_map/finish/pallas_call | solution.py:232
  (64 shorter events, 17.0 us)
Async XLA Ops:
  6.3 30.9 %collective-permute-start = (bf16[256,3328]{1,0:T(8,128)(2,1)S(1)}, bf16[256,3328]{1,0:T(8,128)(2,1)}, u32[]{:S(2)}, u32[]{:S(2)}) collective-permute-start(bf16[256,3328]{1,0:T(8,128)(2,1)S(1)} %get-tuple-element.17.s_ref), channel_id=1, source_target_pairs={{0,8},{8,0},{16,24},{24,16},{32,40},{40,32},{48,56},{56,48},{64,72... | collective-permute-start | bytes 5111816 | tf_op jit(solution)/shard_map/ppermute | solution.py:286
  7.1 5.4 %collective-permute-start.1 = (f32[128,256]{1,0:T(8,128)S(1)}, f32[128,256]{1,0:T(8,128)S(1)}, u32[]{:S(2)}, u32[]{:S(2)}) collective-permute-start(f32[128,256]{1,0:T(8,128)S(1)} %constant_dynamic-slice_fusion), channel_id=1, source_target_pairs={{0,1},{1,0},{2,3},{3,2},{4,5},{5,4},{6,7},{7,6},{8,9},{9,8},{10,11... | collective-permute-start | bytes 393224 | tf_op jit(solution)/shard_map/ppermute | solution.py:260
  12.5 4.6 %collective-permute-start.2 = (f32[64,256]{1,0:T(8,128)S(1)}, f32[64,256]{1,0:T(8,128)S(1)}, u32[]{:S(2)}, u32[]{:S(2)}) collective-permute-start(f32[64,256]{1,0:T(8,128)S(1)} %dynamic-slice_add_fusion), channel_id=1, source_target_pairs={{0,2},{1,3},{2,0},{3,1},{4,6},{5,7},{6,4},{7,5},{8,10},{9,11},{10,... | collective-permute-start | bytes 196616 | tf_op jit(solution)/shard_map/ppermute | solution.py:261
  17.1 6.9 %collective-permute-start.3 = (f32[64,256]{1,0:T(8,128)S(1)}, f32[64,256]{1,0:T(8,128)S(1)}, u32[]{:S(2)}, u32[]{:S(2)}) collective-permute-start(f32[64,256]{1,0:T(8,128)S(1)} %add_add_fusion.6), channel_id=1, source_target_pairs={{0,7},{1,6},{2,5},{3,4},{4,3},{5,2},{6,1},{7,0},{8,15},{9,14},{10,... | collective-permute-start | bytes 196616 | tf_op jit(solution)/shard_map/ppermute | solution.py:267
  24.0 4.2 %collective-permute-start.4 = (f32[64,256]{1,0:T(8,128)S(1)}, f32[64,256]{1,0:T(8,128)S(1)}, u32[]{:S(2)}, u32[]{:S(2)}) collective-permute-start(f32[64,256]{1,0:T(8,128)S(1)} %add.207.refs_0_), channel_id=1, source_target_pairs={{0,2},{1,3},{2,0},{3,1},{4,6},{5,7},{6,4},{7,5},{8,10},{9,11},{10,... | collective-permute-start | bytes 196616 | tf_op jit(solution)/shard_map/ppermute | solution.py:261
  25.5 8.4 %collective-permute-start.5 = (f32[64,256]{1,0:T(8,128)S(1)}, f32[64,256]{1,0:T(8,128)S(1)}, u32[]{:S(2)}, u32[]{:S(2)}) collective-permute-start(f32[64,256]{1,0:T(8,128)S(1)} %add.207.refs_0_), channel_id=1, source_target_pairs={{0,1},{1,0},{2,3},{3,2},{4,5},{5,4},{6,7},{7,6},{8,9},{9,8},{10,11... | collective-permute-start | bytes 196616 | tf_op jit(solution)/shard_map/ppermute | solution.py:260
  28.2 6.2 %collective-permute-start.6 = (f32[64,256]{1,0:T(8,128)S(1)}, f32[64,256]{1,0:T(8,128)S(1)}, u32[]{:S(2)}, u32[]{:S(2)}) collective-permute-start(f32[64,256]{1,0:T(8,128)S(1)} %collective-permute-done.4.refs_1_), channel_id=1, source_target_pairs={{0,1},{1,0},{2,3},{3,2},{4,5},{5,4},{6,7},{7,6},{8,9},{9,8},{10,11... | collective-permute-start | bytes 196616 | tf_op jit(solution)/shard_map/ppermute | solution.py:260
  29.8 6.6 %collective-permute-start.7 = (f32[64,256]{1,0:T(8,128)S(1)}, f32[64,256]{1,0:T(8,128)S(1)}, u32[]{:S(2)}, u32[]{:S(2)}) collective-permute-start(f32[64,256]{1,0:T(8,128)S(1)} %add.207.refs_0_), channel_id=1, source_target_pairs={{0,8},{8,0},{16,24},{24,16},{32,40},{40,32},{48,56},{56,48},{64,72... | collective-permute-start | bytes 196616 | tf_op jit(solution)/shard_map/ppermute | solution.py:288
  34.0 2.4 %collective-permute-start.8 = (f32[64,256]{1,0:T(8,128)S(1)}, f32[64,256]{1,0:T(8,128)S(1)}, u32[]{:S(2)}, u32[]{:S(2)}) collective-permute-start(f32[64,256]{1,0:T(8,128)S(1)} %collective-permute-done.4.refs_1_), channel_id=1, source_target_pairs={{0,8},{8,0},{16,24},{24,16},{32,40},{40,32},{48,56},{56,48},{64,72... | collective-permute-start | bytes 196616 | tf_op jit(solution)/shard_map/ppermute | solution.py:288
  34.0 2.4 %collective-permute-start.9 = (f32[64,256]{1,0:T(8,128)S(1)}, f32[64,256]{1,0:T(8,128)S(1)}, u32[]{:S(2)}, u32[]{:S(2)}) collective-permute-start(f32[64,256]{1,0:T(8,128)S(1)} %collective-permute-done.5.refs_2_), channel_id=1, source_target_pairs={{0,8},{8,0},{16,24},{24,16},{32,40},{40,32},{48,56},{56,48},{64,72... | collective-permute-start | bytes 196616 | tf_op jit(solution)/shard_map/ppermute | solution.py:288
  34.5 2.7 %collective-permute-start.10 = (f32[64,256]{1,0:T(8,128)S(1)}, f32[64,256]{1,0:T(8,128)S(1)}, u32[]{:S(2)}, u32[]{:S(2)}) collective-permute-start(f32[64,256]{1,0:T(8,128)S(1)} %collective-permute-done.6.refs_3_), channel_id=1, source_target_pairs={{0,8},{8,0},{16,24},{24,16},{32,40},{40,32},{48,56},{56,48},{64,72... | collective-permute-start | bytes 196616 | tf_op jit(solution)/shard_map/ppermute | solution.py:288
  41.9 8.1 %collective-permute-start.13 = (f32[128,256]{1,0:T(8,128)S(1)}, f32[128,256]{1,0:T(8,128)S(1)}, u32[]{:S(2)}, u32[]{:S(2)}) collective-permute-start(f32[128,256]{1,0:T(8,128)S(1)} %get-tuple-element.19), channel_id=1, source_target_pairs={{0,192},{8,200},{16,208},{24,216},{32,224},{40,232},{48,240},{56,2... | collective-permute-start | bytes 393224 | tf_op jit(solution)/shard_map/ppermute | solution.py:37
  44.5 14.3 %collective-permute-start.14 = (f32[832,128]{1,0:T(8,128)S(1)}, f32[832,128]{1,0:T(8,128)S(1)}, u32[]{:S(2)}, u32[]{:S(2)}) collective-permute-start(f32[832,128]{1,0:T(8,128)S(1)} %get-tuple-element.22), channel_id=1, source_target_pairs={{0,32},{8,40},{16,48},{24,56},{32,0},{40,8},{48,16},{56,24},{64,96... | collective-permute-start | bytes 1277960 | tf_op jit(solution)/shard_map/ppermute | solution.py:296
  47.4 19.5 %collective-permute-start.15 = (f32[832,128]{1,0:T(8,128)S(1)}, f32[832,128]{1,0:T(8,128)S(1)}, u32[]{:S(2)}, u32[]{:S(2)}) collective-permute-start(f32[832,128]{1,0:T(8,128)S(1)} %get-tuple-element.23), channel_id=1, source_target_pairs={{0,16},{8,24},{16,32},{24,40},{32,48},{40,56},{48,0},{56,8},{64,80... | collective-permute-start | bytes 1277960 | tf_op jit(solution)/shard_map/ppermute | solution.py:296
  47.8 19.1 %collective-permute-start.16 = (f32[832,128]{1,0:T(8,128)S(1)}, f32[832,128]{1,0:T(8,128)S(1)}, u32[]{:S(2)}, u32[]{:S(2)}) collective-permute-start(f32[832,128]{1,0:T(8,128)S(1)} %get-tuple-element.24), channel_id=1, source_target_pairs={{0,48},{8,56},{16,0},{24,8},{32,16},{40,24},{48,32},{56,40},{64,11... | collective-permute-start | bytes 1277960 | tf_op jit(solution)/shard_map/ppermute | solution.py:296
  50.1 7.2 %collective-permute-start.12 = (f32[128,256]{1,0:T(8,128)S(1)}, f32[128,256]{1,0:T(8,128)S(1)}, u32[]{:S(2)}, u32[]{:S(2)}) collective-permute-start(f32[128,256]{1,0:T(8,128)S(1)} %get-tuple-element.19), channel_id=1, source_target_pairs={{0,64},{8,72},{16,80},{24,88},{32,96},{40,104},{48,112},{56,120},{... | collective-permute-start | bytes 393224 | tf_op jit(solution)/shard_map/ppermute | solution.py:37
  50.1 7.2 %collective-permute-start.11 = (f32[128,256]{1,0:T(8,128)S(1)}, f32[128,256]{1,0:T(8,128)S(1)}, u32[]{:S(2)}, u32[]{:S(2)}) collective-permute-start(f32[128,256]{1,0:T(8,128)S(1)} %get-tuple-element.19), channel_id=1, source_target_pairs={{0,128},{8,136},{16,144},{24,152},{32,160},{40,168},{48,176},{56,1... | collective-permute-start | bytes 393224 | tf_op jit(solution)/shard_map/ppermute | solution.py:37
  57.3 12.2 %collective-permute-start.23 = (f32[128,256]{1,0:T(8,128)S(1)}, f32[128,256]{1,0:T(8,128)S(1)}, u32[]{:S(2)}, u32[]{:S(2)}) collective-permute-start(f32[128,256]{1,0:T(8,128)S(1)} %add_add_fusion.1), channel_id=1, source_target_pairs={{0,48},{8,56},{16,0},{24,8},{32,16},{40,24},{48,32},{56,40},{64,11... | collective-permute-start | bytes 393224 | tf_op jit(solution)/shard_map/ppermute | solution.py:37
  57.4 13.3 %collective-permute-start.22 = (f32[128,256]{1,0:T(8,128)S(1)}, f32[128,256]{1,0:T(8,128)S(1)}, u32[]{:S(2)}, u32[]{:S(2)}) collective-permute-start(f32[128,256]{1,0:T(8,128)S(1)} %add_add_fusion.1), channel_id=1, source_target_pairs={{0,16},{8,24},{16,32},{24,40},{32,48},{40,56},{48,0},{56,8},{64,80... | collective-permute-start | bytes 393224 | tf_op jit(solution)/shard_map/ppermute | solution.py:37
  58.8 12.7 %collective-permute-start.21 = (f32[128,256]{1,0:T(8,128)S(1)}, f32[128,256]{1,0:T(8,128)S(1)}, u32[]{:S(2)}, u32[]{:S(2)}) collective-permute-start(f32[128,256]{1,0:T(8,128)S(1)} %add_add_fusion.1), channel_id=1, source_target_pairs={{0,32},{8,40},{16,48},{24,56},{32,0},{40,8},{48,16},{56,24},{64,96... | collective-permute-start | bytes 393224 | tf_op jit(solution)/shard_map/ppermute | solution.py:37
  67.0 6.2 %collective-permute-start.17 = (f32[208,128]{1,0:T(8,128)S(1)}, f32[208,128]{1,0:T(8,128)S(1)}, u32[]{:S(2)}, u32[]{:S(2)}) collective-permute-start(f32[208,128]{1,0:T(8,128)S(1)} %get-tuple-element.31), channel_id=1, source_target_pairs={{0,128},{8,136},{16,144},{24,152},{32,160},{40,168},{48,176},{56,1... | collective-permute-start | bytes 319496 | tf_op jit(solution)/shard_map/ppermute | solution.py:304
  67.6 5.6 %collective-permute-start.19 = (f32[208,128]{1,0:T(8,128)S(1)}, f32[208,128]{1,0:T(8,128)S(1)}, u32[]{:S(2)}, u32[]{:S(2)}) collective-permute-start(f32[208,128]{1,0:T(8,128)S(1)} %get-tuple-element.32), channel_id=1, source_target_pairs={{0,192},{8,200},{16,208},{24,216},{32,224},{40,232},{48,240},{56,2... | collective-permute-start | bytes 319496 | tf_op jit(solution)/shard_map/ppermute | solution.py:305
  69.5 5.9 %collective-permute-start.18 = (f32[208,128]{1,0:T(8,128)S(1)}, f32[208,128]{1,0:T(8,128)S(1)}, u32[]{:S(2)}, u32[]{:S(2)}) collective-permute-start(f32[208,128]{1,0:T(8,128)S(1)} %get-tuple-element.33), channel_id=1, source_target_pairs={{0,64},{8,72},{16,80},{24,88},{32,96},{40,104},{48,112},{56,120},{... | collective-permute-start | bytes 319496 | tf_op jit(solution)/shard_map/ppermute | solution.py:305
  71.6 6.2 %collective-permute-start.24 = (f32[128,256]{1,0:T(8,128)S(1)}, f32[128,256]{1,0:T(8,128)S(1)}, u32[]{:S(2)}, u32[]{:S(2)}) collective-permute-start(f32[128,256]{1,0:T(8,128)S(1)} %add_add_fusion.own_ref), channel_id=1, source_target_pairs={{0,8},{8,0},{16,24},{24,16},{32,40},{40,32},{48,56},{56,48},{64,72... | collective-permute-start | bytes 393224 | tf_op jit(solution)/shard_map/ppermute | solution.py:306
  75.4 52.4 %collective-permute-start.20 = (f32[208,128]{1,0:T(8,128)S(1)}, f32[208,128]{1,0:T(8,128)S(1)}, u32[]{:S(2)}, u32[]{:S(2)}) collective-permute-start(f32[208,128]{1,0:T(8,128)S(1)} %add_add_fusion.2), channel_id=1, source_target_pairs={{0,8},{8,0},{16,24},{24,16},{32,40},{40,32},{48,56},{56,48},{64,72... | collective-permute-start | bytes 319496 | tf_op jit(solution)/shard_map/ppermute | solution.py:307
  128.3 31.6 %copy-start.4 = (bf16[256,3328]{1,0:T(8,128)(2,1)S(1)}, bf16[256,3328]{1,0:T(8,128)(2,1)}, u32[]{:S(2)}) copy-start(bf16[256,3328]{1,0:T(8,128)(2,1)} %g_ref.1) | copy-start | bytes 5111812
  128.4 31.4 %copy-start.2 = (bf16[256,3328]{1,0:T(8,128)(2,1)S(1)}, bf16[256,3328]{1,0:T(8,128)(2,1)}, u32[]{:S(2)}) copy-start(bf16[256,3328]{1,0:T(8,128)(2,1)} %m_ref.1) | copy-start | bytes 5111812
  146.9 13.0 %collective-permute-start.28 = (bf16[3328,128]{1,0:T(8,128)(2,1)S(1)}, bf16[3328,128]{1,0:T(8,128)(2,1)S(1)}, u32[]{:S(2)}, u32[]{:S(2)}) collective-permute-start(bf16[3328,128]{1,0:T(8,128)(2,1)S(1)} %bitcast.10), channel_id=1, source_target_pairs={{0,8},{8,0},{16,24},{24,16},{32,40},{40,32},{48,56},{56,48},{64,72... | collective-permute-start | bytes 2555912 | tf_op jit(solution)/shard_map/ppermute | solution.py:316
  148.7 2.7 %collective-permute-start.25 = (f32[1,128]{1,0:T(1,128)S(1)}, f32[1,128]{1,0:T(1,128)S(1)}, u32[]{:S(2)}, u32[]{:S(2)}) collective-permute-start(f32[1,128]{1,0:T(1,128)S(1)} %bitcast.13), channel_id=1, source_target_pairs={{0,1},{1,0},{2,3},{3,2},{4,5},{5,4},{6,7},{7,6},{8,9},{9,8},{10,11... | collective-permute-start | bytes 1544 | tf_op jit(solution)/shard_map/ppermute | solution.py:322
  151.4 3.3 %collective-permute-start.26 = (f32[1,128]{1,0:T(1,128)S(1)}, f32[1,128]{1,0:T(1,128)S(1)}, u32[]{:S(2)}, u32[]{:S(2)}) collective-permute-start(f32[1,128]{1,0:T(1,128)S(1)} %bitcast_add_fusion), channel_id=1, source_target_pairs={{0,2},{1,3},{2,0},{3,1},{4,6},{5,7},{6,4},{7,5},{8,10},{9,11},{10,... | collective-permute-start | bytes 1544 | tf_op jit(solution)/shard_map/ppermute | solution.py:322
  154.7 7.5 %collective-permute-start.27 = (f32[1,128]{1,0:T(1,128)S(1)}, f32[1,128]{1,0:T(1,128)S(1)}, u32[]{:S(2)}, u32[]{:S(2)}) collective-permute-start(f32[1,128]{1,0:T(1,128)S(1)} %add.242), channel_id=1, source_target_pairs={{0,7},{1,6},{2,5},{3,4},{4,3},{5,2},{6,1},{7,0},{8,15},{9,14},{10,... | collective-permute-start | bytes 1544 | tf_op jit(solution)/shard_map/ppermute | solution.py:322
  162.2 3.4 %collective-permute-start.29 = (f32[1,128]{1,0:T(1,128)S(1)}, f32[1,128]{1,0:T(1,128)S(1)}, u32[]{:S(2)}, u32[]{:S(2)}) collective-permute-start(f32[1,128]{1,0:T(1,128)S(1)} %add.244), channel_id=1, source_target_pairs={{0,8},{8,0},{16,24},{24,16},{32,40},{40,32},{48,56},{56,48},{64,72... | collective-permute-start | bytes 1544 | tf_op jit(solution)/shard_map/ppermute | solution.py:326
  (4 other events, 15.3 us)
